TPU v7x, 512 devices: a whole 4x8x8 slice. The times are simulated.
512 devices in a mesh: src: 8 (over x, y_lo), gx: 16 (over z, core), gy: 4 (over y_hi).
Axes of the slice: x: 4, y: 8 (y_hi: 4, y_lo: 2; y = y_hi * 2 + y_lo), z: 8, core: 2. Of those that a mesh axis runs over, the one named last changes fastest.
Arguments:
- warm_potential: float32 [32, 64, 128, 128], P('src', 'gx', 'gy'), may hold values from -3 to 3
- warm_adjoint: float32 [32, 64, 128, 128], P('src', 'gx', 'gy'), may hold values from -3 to 3
- conductivity: float32 [64, 128, 128], P('gx', 'gy', 'src'), may hold values from 0.2 to 5
- electrodes: int32 [32, 2], replicated, may hold values from 0 to 8191
- receivers: int32 [128, 2], replicated, may hold values from 0 to 8191
- observed: float32 [32, 128], replicated, may hold values from -6 to 6
- source_order: int32 [32], replicated, may hold values from 0 to 31, each once
Outputs:
- gradient: float32 [64, 128, 128], P('gx', 'gy', 'src')
Inputs may be any that keep to these rules, and one draw needn't show every extreme that they name: `electrodes`: entries number surface cells as x * 128 + y. `receivers`: entries number surface cells as x * 128 + y.
All inputs are finite; a program needn't handle non-finite values.
Results may differ from a plain program's by a relative error of at most 0.0003.
Values sent between devices are 32-bit elements; how exact they have to be, the bound alone decides.
A program may use at most 64 MiB of HBM per device.

v0:
```python
import jax
import jax.numpy as jnp
from jax import lax
from jax.sharding import PartitionSpec as P

SWEEPS = 6


lowest = 0.05
highest = 2.0
centre = (highest + lowest) / 2.0
half_span = (highest - lowest) / 2.0
bound_ratio = centre / half_span
strength = 4.0


def padded_2(block, sides, width):
    for axis, dim in sides:
        count = lax.axis_size(axis)
        forward = [(i, i + 1) for i in range(count - 1)]
        backward = [(target, source) for source, target in forward]
        low = lax.ppermute(
            lax.slice_in_dim(block, block.shape[dim] - width, None, axis=dim), axis, forward
        )
        high = lax.ppermute(lax.slice_in_dim(block, 0, width, axis=dim), axis, backward)
        block = jnp.concatenate([low, block, high], axis=dim)
    return block


def harmonic(left, right):
    return jnp.where(right > 0, 2.0 * left * right / (left + right), left)


def slope_of(left, right):
    total = left + right
    return jnp.where(right > 0, 2.0 * right * right / (total * total), 1.0)


def neighbours(field, padded):
    widths = [(0, 0)] * (field.ndim - 1) + [(1, 1)]
    deeper = jnp.pad(field, widths)
    return (
        padded[..., :-2, 1:-1, :],
        padded[..., 2:, 1:-1, :],
        padded[..., 1:-1, :-2, :],
        padded[..., 1:-1, 2:, :],
        deeper[..., :-2],
        deeper[..., 2:],
    )


def face_tables(sigma, padded):
    others = neighbours(sigma, padded)
    depth = lax.broadcasted_iota(jnp.int32, sigma.shape, 2)
    surface = depth == 0
    coeffs = [harmonic(sigma, other) for other in others]
    slopes = [slope_of(sigma, other) for other in others]
    coeffs[4] = jnp.where(surface, 0.0, coeffs[4])
    slopes[4] = jnp.where(surface, 0.0, slopes[4])
    return (coeffs, slopes)


def apply_operator(field, padded, coeffs):
    others = neighbours(field, padded)
    total = coeffs[0] * (field - others[0])
    for index in range(1, 6):
        total = total + coeffs[index] * (field - others[index])
    return total


def solve(rhs, start, coeffs, inverse, pad_fn):
    residual = rhs - apply_operator(start, pad_fn(start), coeffs)
    update = inverse * residual / centre
    iterate = start
    factor = 1.0 / bound_ratio
    for sweep in range(SWEEPS):
        iterate = iterate + update
        residual = residual - apply_operator(update, pad_fn(update), coeffs)
        following = 1.0 / (2.0 * bound_ratio - factor)
        update = following * factor * update + 2.0 * following / half_span * (inverse * residual)
        factor = following
    return iterate + update


def gradient_term(potential, adjoint, padded_potential, padded_adjoint, slopes):
    near_potential = neighbours(potential, padded_potential)
    near_adjoint = neighbours(adjoint, padded_adjoint)
    total = slopes[0] * (potential - near_potential[0]) * (adjoint - near_adjoint[0])
    for index in range(1, 6):
        total = total + slopes[index] * (potential - near_potential[index]) * (
            adjoint - near_adjoint[index]
        )
    return total


def pad_joint(field):
    return padded_2(field, (("gx", 1), ("gy", 2)), 1)


def reduce_groups(partial_value, depth):
    summed = lax.psum(partial_value, "src")
    return lax.dynamic_slice_in_dim(summed, lax.axis_index("src") * depth, depth, 2)


def body(warm_potential, warm_adjoint, conductivity, electrodes, receivers, observed, source_order):
    panel = lax.all_gather(conductivity, "src", axis=2, tiled=True)
    group = lax.axis_index("src")
    slots = warm_potential.shape[0]
    width_x = panel.shape[0]
    ny_global = panel.shape[1] * lax.axis_size("gy")
    x_start = lax.axis_index("gx") * width_x
    potential_start, adjoint_start = (warm_potential, warm_adjoint)
    first_slot = group * slots
    y_start = lax.axis_index("gy") * panel.shape[1]
    width_y = panel.shape[1]
    depth_cells = panel.shape[2]
    coeffs, slopes = face_tables(panel, pad_joint(panel[None])[0])
    inverse = 1.0 / (coeffs[0] + coeffs[1] + coeffs[2] + coeffs[3] + coeffs[4] + coeffs[5])
    idents = lax.dynamic_slice_in_dim(source_order, first_slot, slots)
    pairs = jnp.take(electrodes, idents, axis=0)
    rows_observed = jnp.take(observed, idents, axis=0)

    def picker(cells):
        local_x = cells // ny_global - x_start
        local_y = cells % ny_global - y_start
        inside = (local_x >= 0) & (local_x < width_x) & (local_y >= 0) & (local_y < width_y)
        flat = local_x * width_y + local_y
        places = lax.broadcasted_iota(jnp.int32, (cells.shape[0], width_x * width_y), 1)
        return jnp.where((flat[:, None] == places) & inside[:, None], 1.0, 0.0).astype(jnp.float32)

    def on_surface(flat):
        field = jnp.zeros((slots, width_x, width_y, depth_cells), jnp.float32)
        return field.at[..., 0].set(flat.reshape(slots, width_x, width_y))

    source_surface = strength * (picker(pairs[:, 0]) - picker(pairs[:, 1]))
    potential = solve(on_surface(source_surface), potential_start, coeffs, inverse, pad_joint)
    pickup = picker(receivers[:, 0]) - picker(receivers[:, 1])
    top = potential[..., 0].reshape(slots, width_x * width_y)
    local_values = jnp.dot(
        top, pickup.T, precision=lax.Precision.HIGHEST, preferred_element_type=jnp.float32
    )
    predicted = lax.psum(local_values, ("gx", "gy"))
    misfit = predicted - rows_observed
    back = jnp.dot(
        misfit, pickup, precision=lax.Precision.HIGHEST, preferred_element_type=jnp.float32
    )
    adjoint = solve(on_surface(back), adjoint_start, coeffs, inverse, pad_joint)
    padded_both = pad_joint(jnp.concatenate([potential, adjoint], 0))
    term = gradient_term(potential, adjoint, padded_both[:slots], padded_both[slots:], slopes)
    partial_value = -jnp.sum(term, axis=0)
    return reduce_groups(partial_value, conductivity.shape[2])


def solution(mesh):
    in_specs = (
        P("src", "gx", "gy", None),
        P("src", "gx", "gy", None),
        P("gx", "gy", "src"),
        P(),
        P(),
        P(),
        P(),
    )
    out_specs = P("gx", "gy", "src")
    return jax.shard_map(body, mesh=mesh, in_specs=in_specs, out_specs=out_specs, check_vma=False)
```

profile of v0, /device:TPU:1, one launch (start us, length us, event | category | flops | bytes accessed | tf_op | source)
XLA Modules:
  0.0 588.6 jit_solution(16727907163246744626)
XLA Ops:
  7.3 23.3 %all_gather.3 = f32[4,32,128]{1,0,2:T(4,128)S(1)} all-gather(f32[4,32,16]{1,0,2:T(4,128)S(1)} %copy.69), channel_id=1, replica_groups=mesh['src'=8,'gx'=16,'gy'=4] {'src'}, dimensions={2}, use_global_device_ids=true | all-gather | bytes 73728 | tf_op jit(solution)/shard_map/all_gather | solution.py:106
  30.8 14.2 %collective-permute-start.1 = (f32[1,1,32,128]{2,1,3,0:T(1,128)S(1)}, f32[1,1,32,128]{2,1,3,0:T(1,128)S(1)}, u32[]{:S(2)}, u32[]{:S(2)}) collective-permute-start(f32[1,1,32,128]{2,1,3,0:T(1,128)S(1)} %get-tuple-element.153), channel_id=1, source_target_pairs={{4,0},{8,4},{12,8},{16,12},{20,16},{24,20},{28,24},{32,28},{36,32}... | collective-permute-start | bytes 49160 | tf_op jit(solution)/shard_map/ppermute | solution.py:25
  45.0 1.9 collective-permute-start
  47.0 1.9 collective-permute-start.4
  48.9 2.4 collective-permute-start.5
  56.5 4.9 collective-permute-start.2
  61.5 19.6 %collective-permute-done.3 = f32[1,6,1,128]{2,1,3,0:T(8,128)S(1)} collective-permute-done((f32[1,6,1,128]{2,1,3,0:T(8,128)S(1)}, f32[1,6,1,128]{2,1,3,0:T(8,128)S(1)}, u32[]{:S(2)}, u32[]{:S(2)}) %collective-permute-start.3) | collective-permute-done | bytes 3104 | tf_op jit(solution)/shard_map/ppermute | solution.py:25
  84.8 4.9 collective-permute-start.6
  89.7 2.0 add_divide_fusion
  94.7 2.9 collective-permute-start.9
  97.5 5.0 collective-permute-start.8
  105.1 6.9 %collective-permute-start.10 = (f32[4,6,1,128]{3,2,1,0:T(1,128)S(1)}, f32[4,6,1,128]{3,2,1,0:T(1,128)S(1)}, u32[]{:S(2)}, u32[]{:S(2)}) collective-permute-start(f32[4,6,1,128]{3,2,1,0:T(1,128)S(1)} %get-tuple-element.118), channel_id=1, source_target_pairs={{0,1},{1,2},{2,3},{4,5},{5,6},{6,7},{8,9},{9,10},{10,11},{12,13},{... | collective-permute-start | bytes 36872 | tf_op jit(solution)/shard_map/ppermute | solution.py:22
  113.2 1.9 collective-permute-start.13
  115.1 5.1 collective-permute-start.12
  122.9 6.4 %collective-permute-start.14 = (f32[4,6,1,128]{3,2,1,0:T(1,128)S(1)}, f32[4,6,1,128]{3,2,1,0:T(1,128)S(1)}, u32[]{:S(2)}, u32[]{:S(2)}) collective-permute-start(f32[4,6,1,128]{3,2,1,0:T(1,128)S(1)} %get-tuple-element.116), channel_id=1, source_target_pairs={{0,1},{1,2},{2,3},{4,5},{5,6},{6,7},{8,9},{9,10},{10,11},{12,13},{... | collective-permute-start | bytes 36872 | tf_op jit(solution)/shard_map/ppermute | solution.py:22
  130.4 2.1 collective-permute-start.17
  132.4 5.1 collective-permute-start.16
  140.2 6.7 %collective-permute-start.18 = (f32[4,6,1,128]{3,2,1,0:T(1,128)S(1)}, f32[4,6,1,128]{3,2,1,0:T(1,128)S(1)}, u32[]{:S(2)}, u32[]{:S(2)}) collective-permute-start(f32[4,6,1,128]{3,2,1,0:T(1,128)S(1)} %get-tuple-element.114), channel_id=1, source_target_pairs={{0,1},{1,2},{2,3},{4,5},{5,6},{6,7},{8,9},{9,10},{10,11},{12,13},{... | collective-permute-start | bytes 36872 | tf_op jit(solution)/shard_map/ppermute | solution.py:22
  147.5 4.5 collective-permute-start.32
  152.1 1.9 collective-permute-start.33
  154.3 1.9 collective-permute-start.21
  156.3 3.6 collective-permute-start.20
  163.1 7.3 %collective-permute-start.22 = (f32[4,6,1,128]{3,2,1,0:T(1,128)}, f32[4,6,1,128]{3,2,1,0:T(1,128)}, u32[]{:S(2)}, u32[]{:S(2)}) collective-permute-start(f32[4,6,1,128]{3,2,1,0:T(1,128)} %get-tuple-element.112), channel_id=1, source_target_pairs={{0,1},{1,2},{2,3},{4,5},{5,6},{6,7},{8,9},{9,10},{10,11},{12,13},{... | collective-permute-start | bytes 36872 | tf_op jit(solution)/shard_map/ppermute | solution.py:22
  173.2 1.9 collective-permute-start.25
  175.1 4.5 collective-permute-start.24
  182.3 5.8 collective-permute-start.26
  189.2 1.9 collective-permute-start.29
  191.2 5.1 collective-permute-start.28
  198.9 6.6 %collective-permute-start.30 = (f32[4,6,1,128]{3,2,1,0:T(1,128)S(1)}, f32[4,6,1,128]{3,2,1,0:T(1,128)S(1)}, u32[]{:S(2)}, u32[]{:S(2)}) collective-permute-start(f32[4,6,1,128]{3,2,1,0:T(1,128)S(1)} %get-tuple-element.108), channel_id=1, source_target_pairs={{0,1},{1,2},{2,3},{4,5},{5,6},{6,7},{8,9},{9,10},{10,11},{12,13},{... | collective-permute-start | bytes 36872 | tf_op jit(solution)/shard_map/ppermute | solution.py:22
  206.8 6.7 %collective-permute-start.34 = (f32[4,6,1,128]{3,2,1,0:T(1,128)S(1)}, f32[4,6,1,128]{3,2,1,0:T(1,128)S(1)}, u32[]{:S(2)}, u32[]{:S(2)}) collective-permute-start(f32[4,6,1,128]{3,2,1,0:T(1,128)S(1)} %get-tuple-element.106), channel_id=1, source_target_pairs={{0,1},{1,2},{2,3},{4,5},{5,6},{6,7},{8,9},{9,10},{10,11},{12,13},{... | collective-permute-start | bytes 36872 | tf_op jit(solution)/shard_map/ppermute | solution.py:22
  215.2 141.3 %psum.14 = f32[4,128]{1,0:T(4,128)S(1)} all-reduce(f32[4,128]{1,0:T(4,128)S(1)} %fusion.300), channel_id=1, replica_groups=mesh['src'=8,'gx'=16,'gy'=4] {'gx','gy'}, use_global_device_ids=true, to_apply=%region_0.1 | all-reduce | flops 512 | bytes 4096 | tf_op jit(solution)/shard_map/psum | solution.py:142
  358.1 6.3 %collective-permute-start.37 = (f32[4,1,32,128]{3,2,1,0:T(8,128)S(1)}, f32[4,1,32,128]{3,2,1,0:T(8,128)S(1)}, u32[]{:S(2)}, u32[]{:S(2)}) collective-permute-start(f32[4,1,32,128]{3,2,1,0:T(8,128)S(1)} %get-tuple-element.135), channel_id=1, source_target_pairs={{4,0},{8,4},{12,8},{16,12},{20,16},{24,20},{28,24},{32,28},{36,32}... | collective-permute-start | bytes 196616 | tf_op jit(solution)/shard_map/ppermute | solution.py:25
  369.0 4.9 collective-permute-start.38
  375.0 3.1 collective-permute-start.41
  378.1 4.2 collective-permute-start.40
  385.0 5.4 collective-permute-start.42
  391.6 1.9 collective-permute-start.45
  393.5 5.1 collective-permute-start.44
  401.3 6.6 %collective-permute-start.46 = (f32[4,6,1,128]{3,2,1,0:T(1,128)S(1)}, f32[4,6,1,128]{3,2,1,0:T(1,128)S(1)}, u32[]{:S(2)}, u32[]{:S(2)}) collective-permute-start(f32[4,6,1,128]{3,2,1,0:T(1,128)S(1)} %get-tuple-element.100), channel_id=1, source_target_pairs={{0,1},{1,2},{2,3},{4,5},{5,6},{6,7},{8,9},{9,10},{10,11},{12,13},{... | collective-permute-start | bytes 36872 | tf_op jit(solution)/shard_map/ppermute | solution.py:22
  410.7 5.1 collective-permute-start.48
  418.5 6.7 %collective-permute-start.50 = (f32[4,6,1,128]{3,2,1,0:T(1,128)S(1)}, f32[4,6,1,128]{3,2,1,0:T(1,128)S(1)}, u32[]{:S(2)}, u32[]{:S(2)}) collective-permute-start(f32[4,6,1,128]{3,2,1,0:T(1,128)S(1)} %get-tuple-element.98), channel_id=1, source_target_pairs={{0,1},{1,2},{2,3},{4,5},{5,6},{6,7},{8,9},{9,10},{10,11},{12,13},{... | collective-permute-start | bytes 36872 | tf_op jit(solution)/shard_map/ppermute | solution.py:22
  428.2 5.1 collective-permute-start.52
  435.9 6.7 %collective-permute-start.54 = (f32[4,6,1,128]{3,2,1,0:T(1,128)S(1)}, f32[4,6,1,128]{3,2,1,0:T(1,128)S(1)}, u32[]{:S(2)}, u32[]{:S(2)}) collective-permute-start(f32[4,6,1,128]{3,2,1,0:T(1,128)S(1)} %get-tuple-element.96), channel_id=1, source_target_pairs={{0,1},{1,2},{2,3},{4,5},{5,6},{6,7},{8,9},{9,10},{10,11},{12,13},{... | collective-permute-start | bytes 36872 | tf_op jit(solution)/shard_map/ppermute | solution.py:22
  445.7 5.1 collective-permute-start.56
  453.4 6.7 %collective-permute-start.58 = (f32[4,6,1,128]{3,2,1,0:T(1,128)S(1)}, f32[4,6,1,128]{3,2,1,0:T(1,128)S(1)}, u32[]{:S(2)}, u32[]{:S(2)}) collective-permute-start(f32[4,6,1,128]{3,2,1,0:T(1,128)S(1)} %get-tuple-element.94), channel_id=1, source_target_pairs={{0,1},{1,2},{2,3},{4,5},{5,6},{6,7},{8,9},{9,10},{10,11},{12,13},{... | collective-permute-start | bytes 36872 | tf_op jit(solution)/shard_map/ppermute | solution.py:22
  463.3 5.3 collective-permute-start.60
  472.0 6.7 %collective-permute-start.62 = (f32[8,6,1,128]{3,2,1,0:T(1,128)S(1)}, f32[8,6,1,128]{3,2,1,0:T(1,128)S(1)}, u32[]{:S(2)}, u32[]{:S(2)}) collective-permute-start(f32[8,6,1,128]{3,2,1,0:T(1,128)S(1)} %get-tuple-element.82), channel_id=1, source_target_pairs={{0,1},{1,2},{2,3},{4,5},{5,6},{6,7},{8,9},{9,10},{10,11},{12,13},{... | collective-permute-start | bytes 73736 | tf_op jit(solution)/shard_map/ppermute | solution.py:22
  480.6 99.5 %all-reduce.21.cloned.1.call-done = f32[4,32,128]{2,1,0:T(8,128)} async-done(((f32[4,32,128]{2,1,0:T(8,128)}), f32[4,32,128]{2,1,0:T(8,128)}) %all-reduce.21.cloned.1.call-update) | async-done | bytes 65552 | tf_op jit(solution)/shard_map/psum | solution.py:101
  (219 shorter events, 79.4 us)
Async XLA Ops:
  6.5 573.6 %all-reduce.21.cloned.1.call-start = ((), (), s32[]{:S(2)}) async-start(), calls=%async_computation | async-start | bytes 131072 | tf_op jit(solution)/shard_map/psum | solution.py:101
  30.8 24.0 %collective-permute-start.1 = (f32[1,1,32,128]{2,1,3,0:T(1,128)S(1)}, f32[1,1,32,128]{2,1,3,0:T(1,128)S(1)}, u32[]{:S(2)}, u32[]{:S(2)}) collective-permute-start(f32[1,1,32,128]{2,1,3,0:T(1,128)S(1)} %get-tuple-element.153), channel_id=1, source_target_pairs={{4,0},{8,4},{12,8},{16,12},{20,16},{24,20},{28,24},{32,28},{36,32}... | collective-permute-start | bytes 49160 | tf_op jit(solution)/shard_map/ppermute | solution.py:25
  45.0 9.8 %collective-permute-start = (f32[1,1,32,128]{2,1,3,0:T(1,128)S(1)}, f32[1,1,32,128]{2,1,3,0:T(1,128)S(1)}, u32[]{:S(2)}, u32[]{:S(2)}) collective-permute-start(f32[1,1,32,128]{2,1,3,0:T(1,128)S(1)} %get-tuple-element.152), channel_id=1, source_target_pairs={{0,4},{4,8},{8,12},{12,16},{16,20},{20,24},{24,28},{28,32},{32,36}... | collective-permute-start | bytes 49160 | tf_op jit(solution)/shard_map/ppermute | solution.py:22
  47.0 36.4 %collective-permute-start.4 = (f32[4,1,32,128]{3,2,1,0:T(8,128)S(1)}, f32[4,1,32,128]{3,2,1,0:T(8,128)S(1)}, u32[]{:S(2)}, u32[]{:S(2)}) collective-permute-start(f32[4,1,32,128]{3,2,1,0:T(8,128)S(1)} %get-tuple-element.151), channel_id=1, source_target_pairs={{0,4},{4,8},{8,12},{12,16},{16,20},{20,24},{24,28},{28,32},{32,36}... | collective-permute-start | bytes 196616 | tf_op jit(solution)/shard_map/ppermute | solution.py:22
  48.9 34.6 %collective-permute-start.5 = (f32[4,1,32,128]{3,2,1,0:T(8,128)S(1)}, f32[4,1,32,128]{3,2,1,0:T(8,128)S(1)}, u32[]{:S(2)}, u32[]{:S(2)}) collective-permute-start(f32[4,1,32,128]{3,2,1,0:T(8,128)S(1)} %get-tuple-element.150), channel_id=1, source_target_pairs={{4,0},{8,4},{12,8},{16,12},{20,16},{24,20},{28,24},{32,28},{36,32}... | collective-permute-start | bytes 196616 | tf_op jit(solution)/shard_map/ppermute | solution.py:25
  55.2 25.8 %collective-permute-start.3 = (f32[1,6,1,128]{2,1,3,0:T(8,128)S(1)}, f32[1,6,1,128]{2,1,3,0:T(8,128)S(1)}, u32[]{:S(2)}, u32[]{:S(2)}) collective-permute-start(f32[1,6,1,128]{2,1,3,0:T(8,128)S(1)} %get-tuple-element.93), channel_id=1, source_target_pairs={{1,0},{2,1},{3,2},{5,4},{6,5},{7,6},{9,8},{10,9},{11,10},{13,12},{... | collective-permute-start | bytes 9224 | tf_op jit(solution)/shard_map/ppermute | solution.py:25
  56.5 24.5 %collective-permute-start.2 = (f32[1,6,1,128]{2,1,3,0:T(8,128)S(1)}, f32[1,6,1,128]{2,1,3,0:T(8,128)S(1)}, u32[]{:S(2)}, u32[]{:S(2)}) collective-permute-start(f32[1,6,1,128]{2,1,3,0:T(8,128)S(1)} %get-tuple-element.92), channel_id=1, source_target_pairs={{0,1},{1,2},{2,3},{4,5},{5,6},{6,7},{8,9},{9,10},{10,11},{12,13},{... | collective-permute-start | bytes 9224 | tf_op jit(solution)/shard_map/ppermute | solution.py:22
  83.5 10.0 %collective-permute-start.7 = (f32[4,6,1,128]{3,2,1,0:T(1,128)S(1)}, f32[4,6,1,128]{3,2,1,0:T(1,128)S(1)}, u32[]{:S(2)}, u32[]{:S(2)}) collective-permute-start(f32[4,6,1,128]{3,2,1,0:T(1,128)S(1)} %get-tuple-element.121), channel_id=1, source_target_pairs={{1,0},{2,1},{3,2},{5,4},{6,5},{7,6},{9,8},{10,9},{11,10},{13,12},{... | collective-permute-start | bytes 36872 | tf_op jit(solution)/shard_map/ppermute | solution.py:25
  84.8 8.7 %collective-permute-start.6 = (f32[4,6,1,128]{3,2,1,0:T(1,128)S(1)}, f32[4,6,1,128]{3,2,1,0:T(1,128)S(1)}, u32[]{:S(2)}, u32[]{:S(2)}) collective-permute-start(f32[4,6,1,128]{3,2,1,0:T(1,128)S(1)} %get-tuple-element.120), channel_id=1, source_target_pairs={{0,1},{1,2},{2,3},{4,5},{5,6},{6,7},{8,9},{9,10},{10,11},{12,13},{... | collective-permute-start | bytes 36872 | tf_op jit(solution)/shard_map/ppermute | solution.py:22
  94.7 7.8 %collective-permute-start.9 = (f32[4,1,32,128]{3,2,1,0:T(8,128)S(1)}, f32[4,1,32,128]{3,2,1,0:T(8,128)S(1)}, u32[]{:S(2)}, u32[]{:S(2)}) collective-permute-start(f32[4,1,32,128]{3,2,1,0:T(8,128)S(1)} %get-tuple-element.149), channel_id=1, source_target_pairs={{4,0},{8,4},{12,8},{16,12},{20,16},{24,20},{28,24},{32,28},{36,32}... | collective-permute-start | bytes 196616 | tf_op jit(solution)/shard_map/ppermute | solution.py:25
  103.8 8.2 %collective-permute-start.11 = (f32[4,6,1,128]{3,2,1,0:T(1,128)S(1)}, f32[4,6,1,128]{3,2,1,0:T(1,128)S(1)}, u32[]{:S(2)}, u32[]{:S(2)}) collective-permute-start(f32[4,6,1,128]{3,2,1,0:T(1,128)S(1)} %get-tuple-element.119), channel_id=1, source_target_pairs={{1,0},{2,1},{3,2},{5,4},{6,5},{7,6},{9,8},{10,9},{11,10},{13,12},{... | collective-permute-start | bytes 36872 | tf_op jit(solution)/shard_map/ppermute | solution.py:25
  105.1 7.7 %collective-permute-start.10 = (f32[4,6,1,128]{3,2,1,0:T(1,128)S(1)}, f32[4,6,1,128]{3,2,1,0:T(1,128)S(1)}, u32[]{:S(2)}, u32[]{:S(2)}) collective-permute-start(f32[4,6,1,128]{3,2,1,0:T(1,128)S(1)} %get-tuple-element.118), channel_id=1, source_target_pairs={{0,1},{1,2},{2,3},{4,5},{5,6},{6,7},{8,9},{9,10},{10,11},{12,13},{... | collective-permute-start | bytes 36872 | tf_op jit(solution)/shard_map/ppermute | solution.py:22
  113.2 7.1 %collective-permute-start.13 = (f32[4,1,32,128]{3,2,1,0:T(8,128)S(1)}, f32[4,1,32,128]{3,2,1,0:T(8,128)S(1)}, u32[]{:S(2)}, u32[]{:S(2)}) collective-permute-start(f32[4,1,32,128]{3,2,1,0:T(8,128)S(1)} %get-tuple-element.147), channel_id=1, source_target_pairs={{4,0},{8,4},{12,8},{16,12},{20,16},{24,20},{28,24},{32,28},{36,32}... | collective-permute-start | bytes 196616 | tf_op jit(solution)/shard_map/ppermute | solution.py:25
  121.6 7.7 %collective-permute-start.15 = (f32[4,6,1,128]{3,2,1,0:T(1,128)S(1)}, f32[4,6,1,128]{3,2,1,0:T(1,128)S(1)}, u32[]{:S(2)}, u32[]{:S(2)}) collective-permute-start(f32[4,6,1,128]{3,2,1,0:T(1,128)S(1)} %get-tuple-element.117), channel_id=1, source_target_pairs={{1,0},{2,1},{3,2},{5,4},{6,5},{7,6},{9,8},{10,9},{11,10},{13,12},{... | collective-permute-start | bytes 36872 | tf_op jit(solution)/shard_map/ppermute | solution.py:25
  122.9 7.2 %collective-permute-start.14 = (f32[4,6,1,128]{3,2,1,0:T(1,128)S(1)}, f32[4,6,1,128]{3,2,1,0:T(1,128)S(1)}, u32[]{:S(2)}, u32[]{:S(2)}) collective-permute-start(f32[4,6,1,128]{3,2,1,0:T(1,128)S(1)} %get-tuple-element.116), channel_id=1, source_target_pairs={{0,1},{1,2},{2,3},{4,5},{5,6},{6,7},{8,9},{9,10},{10,11},{12,13},{... | collective-permute-start | bytes 36872 | tf_op jit(solution)/shard_map/ppermute | solution.py:22
  130.4 7.2 %collective-permute-start.17 = (f32[4,1,32,128]{3,2,1,0:T(8,128)S(1)}, f32[4,1,32,128]{3,2,1,0:T(8,128)S(1)}, u32[]{:S(2)}, u32[]{:S(2)}) collective-permute-start(f32[4,1,32,128]{3,2,1,0:T(8,128)S(1)} %get-tuple-element.145), channel_id=1, source_target_pairs={{4,0},{8,4},{12,8},{16,12},{20,16},{24,20},{28,24},{32,28},{36,32}... | collective-permute-start | bytes 196616 | tf_op jit(solution)/shard_map/ppermute | solution.py:25
  138.9 15.1 %collective-permute-start.19 = (f32[4,6,1,128]{3,2,1,0:T(1,128)S(1)}, f32[4,6,1,128]{3,2,1,0:T(1,128)S(1)}, u32[]{:S(2)}, u32[]{:S(2)}) collective-permute-start(f32[4,6,1,128]{3,2,1,0:T(1,128)S(1)} %get-tuple-element.115), channel_id=1, source_target_pairs={{1,0},{2,1},{3,2},{5,4},{6,5},{7,6},{9,8},{10,9},{11,10},{13,12},{... | collective-permute-start | bytes 36872 | tf_op jit(solution)/shard_map/ppermute | solution.py:25
  140.2 13.8 %collective-permute-start.18 = (f32[4,6,1,128]{3,2,1,0:T(1,128)S(1)}, f32[4,6,1,128]{3,2,1,0:T(1,128)S(1)}, u32[]{:S(2)}, u32[]{:S(2)}) collective-permute-start(f32[4,6,1,128]{3,2,1,0:T(1,128)S(1)} %get-tuple-element.114), channel_id=1, source_target_pairs={{0,1},{1,2},{2,3},{4,5},{5,6},{6,7},{8,9},{9,10},{10,11},{12,13},{... | collective-permute-start | bytes 36872 | tf_op jit(solution)/shard_map/ppermute | solution.py:22
  147.5 32.2 %collective-permute-start.32 = (f32[4,1,32,128]{3,2,1,0:T(8,128)}, f32[4,1,32,128]{3,2,1,0:T(8,128)S(1)}, u32[]{:S(2)}, u32[]{:S(2)}) collective-permute-start(f32[4,1,32,128]{3,2,1,0:T(8,128)} %get-tuple-element.137), channel_id=1, source_target_pairs={{0,4},{4,8},{8,12},{12,16},{16,20},{20,24},{24,28},{28,32},{32,36}... | collective-permute-start | bytes 196616 | tf_op jit(solution)/shard_map/ppermute | solution.py:22
  152.1 44.2 %collective-permute-start.33 = (f32[4,1,32,128]{3,2,1,0:T(8,128)}, f32[4,1,32,128]{3,2,1,0:T(8,128)}, u32[]{:S(2)}, u32[]{:S(2)}) collective-permute-start(f32[4,1,32,128]{3,2,1,0:T(8,128)} %get-tuple-element.136), channel_id=1, source_target_pairs={{4,0},{8,4},{12,8},{16,12},{20,16},{24,20},{28,24},{32,28},{36,32}... | collective-permute-start | bytes 196616 | tf_op jit(solution)/shard_map/ppermute | solution.py:25
  161.8 10.3 %collective-permute-start.23 = (f32[4,6,1,128]{3,2,1,0:T(1,128)}, f32[4,6,1,128]{3,2,1,0:T(1,128)}, u32[]{:S(2)}, u32[]{:S(2)}) collective-permute-start(f32[4,6,1,128]{3,2,1,0:T(1,128)} %get-tuple-element.113), channel_id=1, source_target_pairs={{1,0},{2,1},{3,2},{5,4},{6,5},{7,6},{9,8},{10,9},{11,10},{13,12},{... | collective-permute-start | bytes 36872 | tf_op jit(solution)/shard_map/ppermute | solution.py:25
  163.1 9.0 %collective-permute-start.22 = (f32[4,6,1,128]{3,2,1,0:T(1,128)}, f32[4,6,1,128]{3,2,1,0:T(1,128)}, u32[]{:S(2)}, u32[]{:S(2)}) collective-permute-start(f32[4,6,1,128]{3,2,1,0:T(1,128)} %get-tuple-element.112), channel_id=1, source_target_pairs={{0,1},{1,2},{2,3},{4,5},{5,6},{6,7},{8,9},{9,10},{10,11},{12,13},{... | collective-permute-start | bytes 36872 | tf_op jit(solution)/shard_map/ppermute | solution.py:22
  181.0 7.1 %collective-permute-start.27 = (f32[4,6,1,128]{3,2,1,0:T(1,128)S(1)}, f32[4,6,1,128]{3,2,1,0:T(1,128)S(1)}, u32[]{:S(2)}, u32[]{:S(2)}) collective-permute-start(f32[4,6,1,128]{3,2,1,0:T(1,128)S(1)} %get-tuple-element.111), channel_id=1, source_target_pairs={{1,0},{2,1},{3,2},{5,4},{6,5},{7,6},{9,8},{10,9},{11,10},{13,12},{... | collective-permute-start | bytes 36872 | tf_op jit(solution)/shard_map/ppermute | solution.py:25
  182.3 6.6 %collective-permute-start.26 = (f32[4,6,1,128]{3,2,1,0:T(1,128)S(1)}, f32[4,6,1,128]{3,2,1,0:T(1,128)S(1)}, u32[]{:S(2)}, u32[]{:S(2)}) collective-permute-start(f32[4,6,1,128]{3,2,1,0:T(1,128)S(1)} %get-tuple-element.110), channel_id=1, source_target_pairs={{0,1},{1,2},{2,3},{4,5},{5,6},{6,7},{8,9},{9,10},{10,11},{12,13},{... | collective-permute-start | bytes 36872 | tf_op jit(solution)/shard_map/ppermute | solution.py:22
  189.2 7.9 %collective-permute-start.29 = (f32[4,1,32,128]{3,2,1,0:T(8,128)S(1)}, f32[4,1,32,128]{3,2,1,0:T(8,128)S(1)}, u32[]{:S(2)}, u32[]{:S(2)}) collective-permute-start(f32[4,1,32,128]{3,2,1,0:T(8,128)S(1)} %get-tuple-element.139), channel_id=1, source_target_pairs={{4,0},{8,4},{12,8},{16,12},{20,16},{24,20},{28,24},{32,28},{36,32}... | collective-permute-start | bytes 196616 | tf_op jit(solution)/shard_map/ppermute | solution.py:25
  197.6 15.9 %collective-permute-start.31 = (f32[4,6,1,128]{3,2,1,0:T(1,128)S(1)}, f32[4,6,1,128]{3,2,1,0:T(1,128)S(1)}, u32[]{:S(2)}, u32[]{:S(2)}) collective-permute-start(f32[4,6,1,128]{3,2,1,0:T(1,128)S(1)} %get-tuple-element.109), channel_id=1, source_target_pairs={{1,0},{2,1},{3,2},{5,4},{6,5},{7,6},{9,8},{10,9},{11,10},{13,12},{... | collective-permute-start | bytes 36872 | tf_op jit(solution)/shard_map/ppermute | solution.py:25
  198.9 14.6 %collective-permute-start.30 = (f32[4,6,1,128]{3,2,1,0:T(1,128)S(1)}, f32[4,6,1,128]{3,2,1,0:T(1,128)S(1)}, u32[]{:S(2)}, u32[]{:S(2)}) collective-permute-start(f32[4,6,1,128]{3,2,1,0:T(1,128)S(1)} %get-tuple-element.108), channel_id=1, source_target_pairs={{0,1},{1,2},{2,3},{4,5},{5,6},{6,7},{8,9},{9,10},{10,11},{12,13},{... | collective-permute-start | bytes 36872 | tf_op jit(solution)/shard_map/ppermute | solution.py:22
  205.5 151.5 %collective-permute-start.35 = (f32[4,6,1,128]{3,2,1,0:T(1,128)S(1)}, f32[4,6,1,128]{3,2,1,0:T(1,128)S(1)}, u32[]{:S(2)}, u32[]{:S(2)}) collective-permute-start(f32[4,6,1,128]{3,2,1,0:T(1,128)S(1)} %get-tuple-element.107), channel_id=1, source_target_pairs={{1,0},{2,1},{3,2},{5,4},{6,5},{7,6},{9,8},{10,9},{11,10},{13,12},{... | collective-permute-start | bytes 36872 | tf_op jit(solution)/shard_map/ppermute | solution.py:25
  206.8 150.2 %collective-permute-start.34 = (f32[4,6,1,128]{3,2,1,0:T(1,128)S(1)}, f32[4,6,1,128]{3,2,1,0:T(1,128)S(1)}, u32[]{:S(2)}, u32[]{:S(2)}) collective-permute-start(f32[4,6,1,128]{3,2,1,0:T(1,128)S(1)} %get-tuple-element.106), channel_id=1, source_target_pairs={{0,1},{1,2},{2,3},{4,5},{5,6},{6,7},{8,9},{9,10},{10,11},{12,13},{... | collective-permute-start | bytes 36872 | tf_op jit(solution)/shard_map/ppermute | solution.py:22
  358.1 8.2 %collective-permute-start.37 = (f32[4,1,32,128]{3,2,1,0:T(8,128)S(1)}, f32[4,1,32,128]{3,2,1,0:T(8,128)S(1)}, u32[]{:S(2)}, u32[]{:S(2)}) collective-permute-start(f32[4,1,32,128]{3,2,1,0:T(8,128)S(1)} %get-tuple-element.135), channel_id=1, source_target_pairs={{4,0},{8,4},{12,8},{16,12},{20,16},{24,20},{28,24},{32,28},{36,32}... | collective-permute-start | bytes 196616 | tf_op jit(solution)/shard_map/ppermute | solution.py:25
  375.0 7.3 %collective-permute-start.41 = (f32[4,1,32,128]{3,2,1,0:T(8,128)S(1)}, f32[4,1,32,128]{3,2,1,0:T(8,128)S(1)}, u32[]{:S(2)}, u32[]{:S(2)}) collective-permute-start(f32[4,1,32,128]{3,2,1,0:T(8,128)S(1)} %get-tuple-element.133), channel_id=1, source_target_pairs={{4,0},{8,4},{12,8},{16,12},{20,16},{24,20},{28,24},{32,28},{36,32}... | collective-permute-start | bytes 196616 | tf_op jit(solution)/shard_map/ppermute | solution.py:25
  383.7 6.8 %collective-permute-start.43 = (f32[4,6,1,128]{3,2,1,0:T(1,128)S(1)}, f32[4,6,1,128]{3,2,1,0:T(1,128)S(1)}, u32[]{:S(2)}, u32[]{:S(2)}) collective-permute-start(f32[4,6,1,128]{3,2,1,0:T(1,128)S(1)} %get-tuple-element.103), channel_id=1, source_target_pairs={{1,0},{2,1},{3,2},{5,4},{6,5},{7,6},{9,8},{10,9},{11,10},{13,12},{... | collective-permute-start | bytes 36872 | tf_op jit(solution)/shard_map/ppermute | solution.py:25
  391.6 7.1 %collective-permute-start.45 = (f32[4,1,32,128]{3,2,1,0:T(8,128)S(1)}, f32[4,1,32,128]{3,2,1,0:T(8,128)S(1)}, u32[]{:S(2)}, u32[]{:S(2)}) collective-permute-start(f32[4,1,32,128]{3,2,1,0:T(8,128)S(1)} %get-tuple-element.131), channel_id=1, source_target_pairs={{4,0},{8,4},{12,8},{16,12},{20,16},{24,20},{28,24},{32,28},{36,32}... | collective-permute-start | bytes 196616 | tf_op jit(solution)/shard_map/ppermute | solution.py:25
  400.0 7.9 %collective-permute-start.47 = (f32[4,6,1,128]{3,2,1,0:T(1,128)S(1)}, f32[4,6,1,128]{3,2,1,0:T(1,128)S(1)}, u32[]{:S(2)}, u32[]{:S(2)}) collective-permute-start(f32[4,6,1,128]{3,2,1,0:T(1,128)S(1)} %get-tuple-element.101), channel_id=1, source_target_pairs={{1,0},{2,1},{3,2},{5,4},{6,5},{7,6},{9,8},{10,9},{11,10},{13,12},{... | collective-permute-start | bytes 36872 | tf_op jit(solution)/shard_map/ppermute | solution.py:25
  401.3 7.2 %collective-permute-start.46 = (f32[4,6,1,128]{3,2,1,0:T(1,128)S(1)}, f32[4,6,1,128]{3,2,1,0:T(1,128)S(1)}, u32[]{:S(2)}, u32[]{:S(2)}) collective-permute-start(f32[4,6,1,128]{3,2,1,0:T(1,128)S(1)} %get-tuple-element.100), channel_id=1, source_target_pairs={{0,1},{1,2},{2,3},{4,5},{5,6},{6,7},{8,9},{9,10},{10,11},{12,13},{... | collective-permute-start | bytes 36872 | tf_op jit(solution)/shard_map/ppermute | solution.py:22
  408.8 7.1 %collective-permute-start.49 = (f32[4,1,32,128]{3,2,1,0:T(8,128)S(1)}, f32[4,1,32,128]{3,2,1,0:T(8,128)S(1)}, u32[]{:S(2)}, u32[]{:S(2)}) collective-permute-start(f32[4,1,32,128]{3,2,1,0:T(8,128)S(1)} %get-tuple-element.129), channel_id=1, source_target_pairs={{4,0},{8,4},{12,8},{16,12},{20,16},{24,20},{28,24},{32,28},{36,32}... | collective-permute-start | bytes 196616 | tf_op jit(solution)/shard_map/ppermute | solution.py:25
  417.2 8.0 %collective-permute-start.51 = (f32[4,6,1,128]{3,2,1,0:T(1,128)S(1)}, f32[4,6,1,128]{3,2,1,0:T(1,128)S(1)}, u32[]{:S(2)}, u32[]{:S(2)}) collective-permute-start(f32[4,6,1,128]{3,2,1,0:T(1,128)S(1)} %get-tuple-element.99), channel_id=1, source_target_pairs={{1,0},{2,1},{3,2},{5,4},{6,5},{7,6},{9,8},{10,9},{11,10},{13,12},{... | collective-permute-start | bytes 36872 | tf_op jit(solution)/shard_map/ppermute | solution.py:25
  418.5 7.5 %collective-permute-start.50 = (f32[4,6,1,128]{3,2,1,0:T(1,128)S(1)}, f32[4,6,1,128]{3,2,1,0:T(1,128)S(1)}, u32[]{:S(2)}, u32[]{:S(2)}) collective-permute-start(f32[4,6,1,128]{3,2,1,0:T(1,128)S(1)} %get-tuple-element.98), channel_id=1, source_target_pairs={{0,1},{1,2},{2,3},{4,5},{5,6},{6,7},{8,9},{9,10},{10,11},{12,13},{... | collective-permute-start | bytes 36872 | tf_op jit(solution)/shard_map/ppermute | solution.py:22
  426.2 7.1 %collective-permute-start.53 = (f32[4,1,32,128]{3,2,1,0:T(8,128)S(1)}, f32[4,1,32,128]{3,2,1,0:T(8,128)S(1)}, u32[]{:S(2)}, u32[]{:S(2)}) collective-permute-start(f32[4,1,32,128]{3,2,1,0:T(8,128)S(1)} %get-tuple-element.127), channel_id=1, source_target_pairs={{4,0},{8,4},{12,8},{16,12},{20,16},{24,20},{28,24},{32,28},{36,32}... | collective-permute-start | bytes 196616 | tf_op jit(solution)/shard_map/ppermute | solution.py:25
  434.6 8.0 %collective-permute-start.55 = (f32[4,6,1,128]{3,2,1,0:T(1,128)S(1)}, f32[4,6,1,128]{3,2,1,0:T(1,128)S(1)}, u32[]{:S(2)}, u32[]{:S(2)}) collective-permute-start(f32[4,6,1,128]{3,2,1,0:T(1,128)S(1)} %get-tuple-element.97), channel_id=1, source_target_pairs={{1,0},{2,1},{3,2},{5,4},{6,5},{7,6},{9,8},{10,9},{11,10},{13,12},{... | collective-permute-start | bytes 36872 | tf_op jit(solution)/shard_map/ppermute | solution.py:25
  435.9 7.5 %collective-permute-start.54 = (f32[4,6,1,128]{3,2,1,0:T(1,128)S(1)}, f32[4,6,1,128]{3,2,1,0:T(1,128)S(1)}, u32[]{:S(2)}, u32[]{:S(2)}) collective-permute-start(f32[4,6,1,128]{3,2,1,0:T(1,128)S(1)} %get-tuple-element.96), channel_id=1, source_target_pairs={{0,1},{1,2},{2,3},{4,5},{5,6},{6,7},{8,9},{9,10},{10,11},{12,13},{... | collective-permute-start | bytes 36872 | tf_op jit(solution)/shard_map/ppermute | solution.py:22
  443.7 7.1 %collective-permute-start.57 = (f32[4,1,32,128]{3,2,1,0:T(8,128)S(1)}, f32[4,1,32,128]{3,2,1,0:T(8,128)S(1)}, u32[]{:S(2)}, u32[]{:S(2)}) collective-permute-start(f32[4,1,32,128]{3,2,1,0:T(8,128)S(1)} %get-tuple-element.125), channel_id=1, source_target_pairs={{4,0},{8,4},{12,8},{16,12},{20,16},{24,20},{28,24},{32,28},{36,32}... | collective-permute-start | bytes 196616 | tf_op jit(solution)/shard_map/ppermute | solution.py:25
  452.1 8.0 %collective-permute-start.59 = (f32[4,6,1,128]{3,2,1,0:T(1,128)S(1)}, f32[4,6,1,128]{3,2,1,0:T(1,128)S(1)}, u32[]{:S(2)}, u32[]{:S(2)}) collective-permute-start(f32[4,6,1,128]{3,2,1,0:T(1,128)S(1)} %get-tuple-element.95), channel_id=1, source_target_pairs={{1,0},{2,1},{3,2},{5,4},{6,5},{7,6},{9,8},{10,9},{11,10},{13,12},{... | collective-permute-start | bytes 36872 | tf_op jit(solution)/shard_map/ppermute | solution.py:25
  453.4 7.5 %collective-permute-start.58 = (f32[4,6,1,128]{3,2,1,0:T(1,128)S(1)}, f32[4,6,1,128]{3,2,1,0:T(1,128)S(1)}, u32[]{:S(2)}, u32[]{:S(2)}) collective-permute-start(f32[4,6,1,128]{3,2,1,0:T(1,128)S(1)} %get-tuple-element.94), channel_id=1, source_target_pairs={{0,1},{1,2},{2,3},{4,5},{5,6},{6,7},{8,9},{9,10},{10,11},{12,13},{... | collective-permute-start | bytes 36872 | tf_op jit(solution)/shard_map/ppermute | solution.py:22
  461.4 7.8 %collective-permute-start.61 = (f32[8,1,32,128]{3,2,1,0:T(8,128)S(1)}, f32[8,1,32,128]{3,2,1,0:T(8,128)S(1)}, u32[]{:S(2)}, u32[]{:S(2)}) collective-permute-start(f32[8,1,32,128]{3,2,1,0:T(8,128)S(1)} %get-tuple-element.91), channel_id=1, source_target_pairs={{4,0},{8,4},{12,8},{16,12},{20,16},{24,20},{28,24},{32,28},{36,32}... | collective-permute-start | bytes 393224 | tf_op jit(solution)/shard_map/ppermute | solution.py:25
  463.3 7.2 %collective-permute-start.60 = (f32[8,1,32,128]{3,2,1,0:T(8,128)S(1)}, f32[8,1,32,128]{3,2,1,0:T(8,128)S(1)}, u32[]{:S(2)}, u32[]{:S(2)}) collective-permute-start(f32[8,1,32,128]{3,2,1,0:T(8,128)S(1)} %get-tuple-element.90), channel_id=1, source_target_pairs={{0,4},{4,8},{8,12},{12,16},{16,20},{20,24},{24,28},{28,32},{32,36}... | collective-permute-start | bytes 393224 | tf_op jit(solution)/shard_map/ppermute | solution.py:22
  470.5 8.8 %collective-permute-start.63 = (f32[8,6,1,128]{3,2,1,0:T(1,128)S(1)}, f32[8,6,1,128]{3,2,1,0:T(1,128)S(1)}, u32[]{:S(2)}, u32[]{:S(2)}) collective-permute-start(f32[8,6,1,128]{3,2,1,0:T(1,128)S(1)} %get-tuple-element.83), channel_id=1, source_target_pairs={{1,0},{2,1},{3,2},{5,4},{6,5},{7,6},{9,8},{10,9},{11,10},{13,12},{... | collective-permute-start | bytes 73736 | tf_op jit(solution)/shard_map/ppermute | solution.py:25
  472.0 7.6 %collective-permute-start.62 = (f32[8,6,1,128]{3,2,1,0:T(1,128)S(1)}, f32[8,6,1,128]{3,2,1,0:T(1,128)S(1)}, u32[]{:S(2)}, u32[]{:S(2)}) collective-permute-start(f32[8,6,1,128]{3,2,1,0:T(1,128)S(1)} %get-tuple-element.82), channel_id=1, source_target_pairs={{0,1},{1,2},{2,3},{4,5},{5,6},{6,7},{8,9},{9,10},{10,11},{12,13},{... | collective-permute-start | bytes 73736 | tf_op jit(solution)/shard_map/ppermute | solution.py:22
  (38 other events, 808.4 us)
Sparse Core Ops, SparseCore 0:
  480.7 99.3 all-reduce.20
where the time goes:
time: 595 us; the launch traced here: 589 us
  starting transfers between devices  239 us (40%)
  blocking collectives  165 us (28%)
  waiting for transfers between devices  143 us (24%)
  other arithmetic  15 us (3%)
  between operations  14.6 us (2%)
  local copies, waits for them, and re-layouts  12.1 us (2%)
    ppermute x32, starting transfers between devices, padded_2(): lax.ppermute(lax.slice_in_dim(block, block.shape[dim] - width, None, axis...  168 us
    psum x1, blocking collectives, body(): predicted = lax.psum(local_values, ('gx', 'gy'))  141 us
    psum x1, waiting for transfers between devices, reduce_groups(): summed = lax.psum(partial_value, 'src')  99.5 us
    ppermute x32, starting transfers between devices, padded_2(): lax.ppermute(lax.slice_in_dim(block, 0, width, axis=dim), axis, backward)  71 us
    all_gather x1, blocking collectives, body(): panel = lax.all_gather(conductivity, 'src', axis=2, tiled=True)  23.3 us
    ppermute x32, waiting for transfers between devices, padded_2(): lax.ppermute(lax.slice_in_dim(block, block.shape[dim] - width, None, axis...  22.8 us
    ppermute x32, waiting for transfers between devices, padded_2(): lax.ppermute(lax.slice_in_dim(block, 0, width, axis=dim), axis, backward)  20.3 us
  transfers between devices with their start and end apart: 65, of which 26 were waited for; matrix products, arithmetic and copies ran while one was open for 3% of the time, Pallas kernels for 0%

commit v1 on v0

v1 whole, which is shorter than its diff:
```python
import functools

import jax
import jax.numpy as jnp
from jax import lax
from jax.experimental import pallas as pl
from jax.experimental.pallas import tpu as pltpu
from jax.sharding import PartitionSpec as P

MESH = pl.DeviceIdType.MESH
SWEEPS = 6
lowest = 0.05
highest = 2.0
centre = (highest + lowest) / 2.0
half_span = (highest - lowest) / 2.0
bound_ratio = centre / half_span
strength = 4.0

F32 = jnp.float32
I32 = jnp.int32
BF16 = jnp.bfloat16

NSRCG, NGX, NGY = 8, 16, 4
NZC = NGX // 2
NX, NY = 64, 128
XR, YR = 4, 32
CX = 2 * XR
HALO = 8
EX, EY = CX + 2 * HALO, YR + 2 * HALO


def chebyshev():
    out = []
    factor = 1.0 / bound_ratio
    for _ in range(SWEEPS):
        following = 1.0 / (2.0 * bound_ratio - factor)
        out.append((following * factor, 2.0 * following / half_span))
        factor = following
    return out


STEPS = chebyshev()


def split3(v):
    hi = v.astype(BF16)
    rest = v - hi.astype(F32)
    mid = rest.astype(BF16)
    lo = (rest - mid.astype(F32)).astype(BF16)
    return hi, mid, lo


def kernel(
    wp_ref, wa_ref, cond_ref, elec_ref, rec_ref, obs_ref, order_ref,
    out_ref,
    p0, p1, a0, a1, cext, coef, slope, gath, pan, pick, pick_own,
    scond, scoef, sinv, srhs, y0, y1, vm, zbuf, gbuf, gt, rbuf,
    loc_sem, warm_s, warm_r, cond_s, cond_r, src_s, src_r, z_s, z_r, g_s, g_r, rs_s, rs_r,
):
    src = lax.axis_index("src")
    gx = lax.axis_index("gx")
    gy = lax.axis_index("gy")
    zc = gx // 2
    core = gx - 2 * zc

    def place(ds=0, dz=0, t=0, dg=0):
        z2 = lax.rem(zc + (dz % NZC), NZC)
        c2 = core if t == 0 else 1 - core
        return {
            "src": lax.rem(src + (ds % NSRCG), NSRCG),
            "gx": 2 * z2 + c2,
            "gy": lax.rem(gy + (dg % NGY), NGY),
        }

    halo = [
        (dz, t, dg)
        for dg in (0, 1, -1)
        for dz in (0, 1, -1)
        for t in (1, 0)
        if (dz, t, dg) != (0, 0, 0)
    ]

    partners = [place(dz=dz, t=t, dg=dg) for dz, t, dg in halo]
    partners += [place(ds=ds, t=t) for ds in range(1, NSRCG) for t in (0, 1)]
    partners += [place(dz=dz) for dz in range(2, NZC - 1)]
    partners += [place(dg=dg) for dg in range(2, NGY - 1)]
    barrier = pltpu.get_barrier_semaphore()
    for device in partners:
        pl.semaphore_signal(barrier, inc=1, device_id=device, device_id_type=MESH)

    own_x = pl.ds(HALO + XR * core, XR)
    half = pl.ds(2 * core, 2)
    own_p = pltpu.make_async_copy(wp_ref.at[half], p0.at[:, own_x, HALO : HALO + YR, :], loc_sem.at[0])
    own_a = pltpu.make_async_copy(wa_ref.at[half], a0.at[:, own_x, HALO : HALO + YR, :], loc_sem.at[1])
    own_p.start()
    own_a.start()

    own_rows = pl.ds(pl.multiple_of(16 * src, 16), 16)
    gath[own_rows, :] = cond_ref[...]

    pl.semaphore_wait(barrier, len(partners))

    gathers = [
        pltpu.make_async_remote_copy(
            cond_ref, gath.at[own_rows, :], src_s.at[ds - 1], src_r.at[ds - 1],
            device_id=place(ds=ds), device_id_type=MESH,
        )
        for ds in range(1, NSRCG)
    ]
    for copy in gathers:
        copy.start()

    def y_spans(dg):
        if dg == 0:
            return slice(0, YR), slice(HALO, HALO + YR)
        if dg == 1:
            return slice(YR - HALO, YR), slice(0, HALO)
        return slice(0, HALO), slice(HALO + YR, EY)

    def warm_copies(which, ref, dest):
        copies = []
        for dz, t, dg in halo:
            ys, yd = y_spans(dg)
            c2 = core if t == 0 else 1 - core
            copies.append(
                pltpu.make_async_remote_copy(
                    ref.at[pl.ds(2 * c2, 2), :, ys, :],
                    dest.at[:, pl.ds(HALO * (1 - dz) + XR * core, XR), yd, :],
                    warm_s.at[which, dz + 1, t, dg + 1],
                    warm_r.at[which, dz + 1, t, dg + 1],
                    device_id=place(dz=dz, t=t, dg=dg), device_id_type=MESH,
                )
            )
        return copies

    copies_p = warm_copies(0, wp_ref, p0)
    copies_a = warm_copies(1, wa_ref, a0)
    for copy in copies_p:
        copy.start()

    rx0 = rec_ref[:, 0:1] >> 7
    ry0 = rec_ref[:, 0:1] & (NY - 1)
    rx1 = rec_ref[:, 1:2] >> 7
    ry1 = rec_ref[:, 1:2] & (NY - 1)

    def own_flat(cx, cy):
        lx = cx - CX * zc
        ly = cy - YR * gy
        inside = (lx >= 0) & (lx < CX) & (ly >= 0) & (ly < YR)
        return jnp.where(inside, lx * YR + ly, -1)

    flats = lax.broadcasted_iota(I32, (128, CX * YR), 1)
    pick_own[...] = (
        jnp.where(own_flat(rx0, ry0) == flats, 1.0, 0.0)
        - jnp.where(own_flat(rx1, ry1) == flats, 1.0, 0.0)
    ).astype(BF16)

    lanes = lax.broadcasted_iota(I32, (128, 128), 1)
    ylane = lanes & 63
    ycell = (YR * gy - HALO + ylane) & (NY - 1)
    ok0 = (ry0 == ycell) & (ylane < EY)
    ok1 = (ry1 == ycell) & (ylane < EY)
    col0 = jnp.where(ok0, rx0, -1)
    col1 = jnp.where(ok1, rx1, -1)
    for r in range(EX):
        xrow = (CX * zc - HALO + r) & (NX - 1)
        pick[:, r * 128 : (r + 1) * 128] = (
            jnp.where(col0 == xrow, 1.0, 0.0) - jnp.where(col1 == xrow, 1.0, 0.0)
        ).astype(BF16)

    for copy in gathers:
        copy.wait_recv()
    pan[...] = jnp.transpose(gath[...]).reshape(XR, YR, 128)
    cext[own_x, HALO : HALO + YR, :] = pan[...]
    copies_c = []
    for dz, t, dg in halo:
        ys, yd = y_spans(dg)
        copies_c.append(
            pltpu.make_async_remote_copy(
                pan.at[:, ys, :],
                cext.at[pl.ds(HALO * (1 - dz) + XR * core, XR), yd, :],
                cond_s.at[dz + 1, t, dg + 1],
                cond_r.at[dz + 1, t, dg + 1],
                device_id=place(dz=dz, t=t, dg=dg), device_id_type=MESH,
            )
        )
    for copy in copies_c:
        copy.start()
    for copy in copies_a:
        copy.start()
    for copy in copies_c:
        copy.wait_recv()

    yy = (YR * gy - HALO + lax.broadcasted_iota(I32, (EY, 128), 0)) & (NY - 1)
    zz = lax.broadcasted_iota(I32, (EY, 128), 1)
    in_ym = yy != 0
    in_yp = yy != NY - 1
    in_zm = zz != 0
    in_zp = zz != 127

    def x_inside(r):
        row = (CX * zc - HALO + r) & (NX - 1)
        return jnp.where(row == 0, 0.0, 1.0).astype(F32), jnp.where(row == NX - 1, 0.0, 1.0).astype(F32)

    def harmonic(s, n):
        return 2.0 * s * n / (s + n)

    def coef_row(r, carry):
        s = cext[r]
        fm, fp = x_inside(r)
        hxm = harmonic(s, cext[r - 1]) * fm
        hxp = harmonic(s, cext[r + 1]) * fp
        hym = jnp.where(in_ym, harmonic(s, pltpu.roll(s, 1, 0)), 0.0)
        hyp = jnp.where(in_yp, harmonic(s, pltpu.roll(s, EY - 1, 0)), 0.0)
        hzm = jnp.where(in_zm, harmonic(s, pltpu.roll(s, 1, 1)), 0.0)
        hzp = jnp.where(in_zp, harmonic(s, pltpu.roll(s, 127, 1)), 0.0)
        diag = hxm + hxp + hym + hyp + hzm + hzp
        diag = diag + s * ((1.0 - fm) + (1.0 - fp))
        diag = diag + jnp.where(in_ym, 0.0, s) + jnp.where(in_yp, 0.0, s) + jnp.where(in_zp, 0.0, s)
        inv = 1.0 / diag
        for i, h in enumerate((hxm, hxp, hym, hyp, hzm, hzp)):
            coef[i, r] = h * inv
        return carry

    lax.fori_loop(1, EX - 1, coef_row, 0)

    def slope_of(s, n):
        total = s + n
        return 2.0 * n * n / (total * total)

    def slope_row(r, carry):
        s = cext[r]
        fm, fp = x_inside(r)
        q = r - HALO
        slope[0, q] = slope_of(s, cext[r - 1]) * fm + (1.0 - fm)
        slope[1, q] = slope_of(s, cext[r + 1]) * fp + (1.0 - fp)
        slope[2, q] = jnp.where(in_ym, slope_of(s, pltpu.roll(s, 1, 0)), 1.0)
        slope[3, q] = jnp.where(in_yp, slope_of(s, pltpu.roll(s, EY - 1, 0)), 1.0)
        slope[4, q] = jnp.where(in_zm, slope_of(s, pltpu.roll(s, 1, 1)), 0.0)
        slope[5, q] = jnp.where(in_zp, slope_of(s, pltpu.roll(s, 127, 1)), 1.0)
        return carry

    for first, count in ((0, 16), (16, 8)):
        gathered = jnp.ones((EY, 128), F32)
        for i in range(count):
            rolled = pltpu.roll(cext[first + i], 8 * i, 1) if i else cext[first]
            gathered = jnp.where((zz >= 8 * i) & (zz < 8 * i + 8), rolled, gathered)
        ones = jnp.ones((64 - EY, 128), F32)
        turned = jnp.transpose(jnp.concatenate([gathered, ones, gathered, ones], axis=0))
        scond[first : first + count] = turned[: 8 * count].reshape(count, 8, 128)

    shape = (EX - 2, 8, 128)
    lane3 = lax.broadcasted_iota(I32, shape, 2)
    sub3 = lax.broadcasted_iota(I32, shape, 1)
    row3 = (lax.broadcasted_iota(I32, shape, 0) + (CX * zc - HALO + 1)) & (NX - 1)
    y3 = (YR * gy - HALO + (lane3 & 63)) & (NY - 1)
    s = scond[1 : EX - 1]
    hs = [
        (harmonic(s, scond[0 : EX - 2]), row3 != 0, True),
        (harmonic(s, scond[2:EX]), row3 != NX - 1, True),
        (harmonic(s, pltpu.roll(s, 1, 2)), y3 != 0, True),
        (harmonic(s, pltpu.roll(s, 127, 2)), y3 != NY - 1, True),
        (harmonic(s, pltpu.roll(s, 1, 1)), sub3 != 0, False),
        (harmonic(s, pltpu.roll(s, 7, 1)), sub3 != 7, False),
    ]
    diag = jnp.zeros(shape, F32)
    for h, inside, outer in hs:
        diag = diag + jnp.where(inside, h, s if outer else 0.0)
    inv = 1.0 / diag
    sinv[...] = inv
    for i, (h, inside, outer) in enumerate(hs):
        scoef[i] = jnp.where(inside, h, 0.0) * inv

    def thin_solve():
        g = sinv[...] * srhs[...]
        zero = jnp.zeros((1, 8, 128), F32)
        for ref in (y0, y1):
            ref[0:1] = zero
            ref[EX - 1 : EX] = zero
        y0[1 : EX - 1] = jnp.zeros(shape, F32)
        y1[1 : EX - 1] = g * (1.0 / centre)
        older, newer = y0, y1
        for a, b in STEPS:
            u = newer[1 : EX - 1]
            total = scoef[0] * newer[0 : EX - 2] + scoef[1] * newer[2:EX]
            total = total + scoef[2] * pltpu.roll(u, 1, 2) + scoef[3] * pltpu.roll(u, 127, 2)
            total = total + scoef[4] * pltpu.roll(u, 1, 1) + scoef[5] * pltpu.roll(u, 7, 1)
            older[1 : EX - 1] = (1.0 + a - b) * u - a * older[1 : EX - 1] + b * (sinv[...] * srhs[...] + total)
            older, newer = newer, older
        return newer

    def add_thin(thin, dest):
        first = HALO - 1
        turned = jnp.transpose(thin[first : first + 16].reshape(128, 128))
        shallow = lanes < 8
        for i in range(CX + 2):
            part = jnp.where(shallow, pltpu.roll(turned, (128 - 8 * i) % 128, 1) if i else turned, 0.0)
            for slot in range(2):
                dest[slot, first + i] = dest[slot, first + i] + part[64 * slot : 64 * slot + EY]

    first_slot = 4 * src + 2 * core
    idents = [order_ref[first_slot + j] for j in range(2)]
    rhs = jnp.zeros(shape, F32)
    for e, sign in ((0, strength), (1, -strength)):
        cells = [elec_ref[k, e] for k in idents]
        ex = jnp.where(lane3 < 64, cells[0] >> 7, cells[1] >> 7)
        ey = jnp.where(lane3 < 64, cells[0] & (NY - 1), cells[1] & (NY - 1))
        hit = (ex == row3) & (ey == y3) & (sub3 == 0) & ((lane3 & 63) < EY)
        rhs = rhs + jnp.where(hit, sign, 0.0)
    srhs[...] = rhs
    thin_p = thin_solve()

    def full_solve(x0, x1):
        def app(x, prev, dest, wc, wu, wp, e):
            def row(r, carry):
                for slot in range(2):
                    u = x[slot, r]
                    total = coef[0, r] * x[slot, r - 1] + coef[1, r] * x[slot, r + 1]
                    total = total + coef[2, r] * pltpu.roll(u, 1, 0) + coef[3, r] * pltpu.roll(u, EY - 1, 0)
                    total = total + coef[4, r] * pltpu.roll(u, 1, 1) + coef[5, r] * pltpu.roll(u, 127, 1)
                    fresh = wu * u + wc * total
                    if prev is not None:
                        fresh = fresh - wp * prev[slot, r]
                    dest[slot, r] = fresh
                return carry

            lax.fori_loop(HALO - e, HALO + CX + e, row, 0)

        app(x0, None, x1, 1.0 / centre, 1.0 - 1.0 / centre, 0.0, HALO - 1)
        older, newer = x0, x1
        for k, (a, b) in enumerate(STEPS):
            app(newer, older, older, b, 1.0 + a - b, a, HALO - 2 - k)
            older, newer = newer, older
        return newer

    own_p.wait()
    for copy in copies_p:
        copy.wait_recv()
    pot = full_solve(p0, p1)
    add_thin(thin_p, pot)

    value = jnp.zeros((128, 128), F32)
    for slot in range(2):
        block = pot[slot, HALO : HALO + CX, HALO : HALO + YR, :].reshape(CX * YR, 128)
        got = jnp.zeros((128, 128), F32)
        for part in split3(block):
            got = got + jnp.dot(pick_own[...], part, preferred_element_type=F32)
        if slot:
            got = pltpu.roll(got, slot, 1)
        value = jnp.where(lanes == slot, got, value)
    vm[0] = jnp.transpose(value)[0:8]
    copies_z = [
        pltpu.make_async_remote_copy(
            vm.at[0], zbuf.at[dz - 1], z_s.at[dz - 1], z_r.at[dz - 1],
            device_id=place(dz=dz), device_id_type=MESH,
        )
        for dz in range(1, NZC)
    ]
    for copy in copies_z:
        copy.start()

    lax.fori_loop(HALO, HALO + CX, slope_row, 0)

    for copy in copies_z:
        copy.wait_recv()
    total = vm[0]
    for i in range(NZC - 1):
        total = total + zbuf[i]
    vm[1] = total
    copies_g = [
        pltpu.make_async_remote_copy(
            vm.at[1], gbuf.at[dg - 1], g_s.at[dg - 1], g_r.at[dg - 1],
            device_id=place(dg=dg), device_id_type=MESH,
        )
        for dg in range(1, NGY)
    ]
    for copy in copies_g:
        copy.start()

    own_a.wait()
    for copy in copies_a:
        copy.wait_recv()
    adj = full_solve(a0, a1)

    for copy in copies_g:
        copy.wait_recv()
    total = vm[1]
    for i in range(NGY - 1):
        total = total + gbuf[i]
    sub8 = lax.broadcasted_iota(I32, (8, 128), 0)
    lane8 = lax.broadcasted_iota(I32, (8, 128), 1)
    seen = jnp.where(sub8 == 0, obs_ref[pl.ds(idents[0], 1), :], obs_ref[pl.ds(idents[1], 1), :])
    misfit = jnp.where(sub8 < 2, total - seen, 0.0)
    hi, mid, lo = split3(misfit)
    stacked = jnp.concatenate(
        [hi.astype(F32), mid.astype(F32), lo.astype(F32), jnp.zeros((8, 128), F32)], axis=0
    ).astype(BF16)
    back = jnp.dot(stacked, pick[...], preferred_element_type=F32)
    for r in range(1, EX - 1):
        cut = back[:, r * 128 : (r + 1) * 128]
        both = cut[0:8] + cut[8:16] + cut[16:24]
        line = jnp.where(lane8[0:1] < 64, both[0:1], both[1:2])
        srhs[r - 1] = jnp.where(sub8 == 0, line, 0.0)
    add_thin(thin_solve(), adj)

    def grad_row(r, carry):
        q = r - HALO
        fm, fp = x_inside(r)
        sums = [jnp.zeros((EY, 128), F32) for _ in range(6)]
        for slot in range(2):
            p = pot[slot, r]
            a = adj[slot, r]
            near = [
                (pot[slot, r - 1] * fm, adj[slot, r - 1] * fm),
                (pot[slot, r + 1] * fp, adj[slot, r + 1] * fp),
            ]
            for inside, shift, axis in ((in_ym, 1, 0), (in_yp, EY - 1, 0), (in_zm, 1, 1), (in_zp, 127, 1)):
                near.append(
                    (
                        jnp.where(inside, pltpu.roll(p, shift, axis), 0.0),
                        jnp.where(inside, pltpu.roll(a, shift, axis), 0.0),
                    )
                )
            sums = [old + (p - pn) * (a - an) for old, (pn, an) in zip(sums, near)]
        out = slope[0, q] * sums[0]
        for i in range(1, 6):
            out = out + slope[i, q] * sums[i]
        pan8[q] = out[HALO : HALO + YR]
        return carry

    pan8 = slope.at[0, :, 0:YR, :]

    def grad_row_stored(r, carry):
        return grad_row(r, carry)

    lax.fori_loop(HALO, HALO + CX, grad_row_stored, 0)
    for c in range(2):
        gt[c] = jnp.transpose(slope[0, XR * c : XR * c + XR, 0:YR, :].reshape(128, 128))

    def rs_copy(ds, t):
        c2 = core if t == 0 else 1 - core
        s2 = lax.rem(src + ds, NSRCG)
        return pltpu.make_async_remote_copy(
            gt.at[c2, pl.ds(pl.multiple_of(16 * s2, 16), 16), :],
            rbuf.at[t, ds],
            rs_s.at[t, ds], rs_r.at[t, ds],
            device_id=place(ds=ds, t=t), device_id_type=MESH,
        )

    copies_rs = [rs_copy(ds, t) for ds in range(NSRCG) for t in (0, 1) if ds or t]
    for copy in copies_rs:
        copy.start()
    for copy in copies_rs:
        copy.wait_recv()
    total = gt[core, own_rows, :]
    for ds in range(NSRCG):
        for t in (0, 1):
            if ds or t:
                total = total + rbuf[t, ds]
    out_ref[...] = -total

    for copies in (gathers, copies_p, copies_a, copies_c, copies_z, copies_g, copies_rs):
        for copy in copies:
            copy.wait_send()


def body(warm_potential, warm_adjoint, conductivity, electrodes, receivers, observed, source_order):
    xr, yr, depth = conductivity.shape
    turned = conductivity.reshape(xr * yr, depth).T
    anyspace = pl.BlockSpec(memory_space=pl.ANY)
    vmem = pl.BlockSpec(memory_space=pltpu.VMEM)
    smem = pl.BlockSpec(memory_space=pltpu.SMEM)
    field = pltpu.VMEM((2, EX, EY, 128), F32)
    thin = pltpu.VMEM((EX, 8, 128), F32)
    inner = pltpu.VMEM((EX - 2, 8, 128), F32)
    dma = pltpu.SemaphoreType.DMA
    result = pl.pallas_call(
        kernel,
        out_shape=jax.ShapeDtypeStruct((16, 128), F32),
        in_specs=[anyspace, anyspace, vmem, smem, vmem, vmem, smem],
        out_specs=vmem,
        scratch_shapes=[
            field, field, field, field,
            pltpu.VMEM((EX, EY, 128), F32),
            pltpu.VMEM((6, EX, EY, 128), F32),
            pltpu.VMEM((6, CX, EY, 128), F32),
            pltpu.VMEM((128, 128), F32),
            pltpu.VMEM((XR, YR, 128), F32),
            pltpu.VMEM((128, EX * 128), BF16),
            pltpu.VMEM((128, CX * YR), BF16),
            thin,
            pltpu.VMEM((6, EX - 2, 8, 128), F32),
            inner, inner, thin, thin,
            pltpu.VMEM((2, 8, 128), F32),
            pltpu.VMEM((NZC - 1, 8, 128), F32),
            pltpu.VMEM((NGY - 1, 8, 128), F32),
            pltpu.VMEM((2, 128, 128), F32),
            pltpu.VMEM((2, NSRCG, 16, 128), F32),
            dma((2,)),
            dma((2, 3, 2, 3)), dma((2, 3, 2, 3)),
            dma((3, 2, 3)), dma((3, 2, 3)),
            dma((NSRCG - 1,)), dma((NSRCG - 1,)),
            dma((NZC - 1,)), dma((NZC - 1,)),
            dma((NGY - 1,)), dma((NGY - 1,)),
            dma((2, NSRCG)), dma((2, NSRCG)),
        ],
        compiler_params=pltpu.CompilerParams(
            collective_id=0, has_side_effects=True, vmem_limit_bytes=40 * 1024 * 1024
        ),
    )(warm_potential, warm_adjoint, turned, electrodes, receivers, observed, source_order)
    return result.T.reshape(xr, yr, depth)


def solution(mesh):
    in_specs = (
        P("src", "gx", "gy", None),
        P("src", "gx", "gy", None),
        P("gx", "gy", "src"),
        P(),
        P(),
        P(),
        P(),
    )
    out_specs = P("gx", "gy", "src")
    return jax.shard_map(body, mesh=mesh, in_specs=in_specs, out_specs=out_specs, check_vma=False)
```

time: 595 us -> 83 us (0.14); the launches traced: 589 us -> 82.7 us
  starting transfers between devices: 239 us -> 0 us
  blocking collectives: 165 us -> 0 us
  waiting for transfers between devices: 143 us -> 0 us
  Pallas kernels: 0 us -> 77 us
  other arithmetic: 15 us -> 0 us
  between operations: 14.6 us -> 0.02 us
  local copies, waits for them, and re-layouts: 12.1 us -> 5.61 us
    ppermute x64 -> x0, starting transfers between devices: 239 us -> none  [the longest x32 168 us: padded_2(): lax.ppermute(lax.slice_in_dim(block, block.shape[dim] - width, None, axis...]
    psum x1 -> x0, blocking collectives: 141 us -> none  [body(): predicted = lax.psum(local_values, ('gx', 'gy'))]
    psum x1 -> x0, waiting for transfers between devices: 99.5 us -> none  [reduce_groups(): summed = lax.psum(partial_value, 'src')]
    pallas_call x0 -> x1, Pallas kernels: none -> 77 us  [body(): pl.pallas_call(kernel, out_shape=jax.ShapeDtypeStruct((16, 128), F32), in...]
    ppermute x64 -> x0, waiting for transfers between devices: 43 us -> none  [the longest x32 22.8 us: padded_2(): lax.ppermute(lax.slice_in_dim(block, block.shape[dim] - width, None, axis...]
    all_gather x1 -> x0, blocking collectives: 23.3 us -> none  [body(): panel = lax.all_gather(conductivity, 'src', axis=2, tiled=True)]
  transfers between devices with their start and end apart: 65 -> 0, of which waited for: 26 -> 0; matrix products, arithmetic and copies ran while one was open for 3% -> 0% of each run, Pallas kernels for 0% -> 0%
where the time goes in v1:
time: 83 us; the launch traced here: 82.7 us
  Pallas kernels  77 us (93%)
  local copies, waits for them, and re-layouts  5.61 us (7%)
    pallas_call x1, Pallas kernels, body(): pl.pallas_call(kernel, out_shape=jax.ShapeDtypeStruct((16, 128), F32), in...  77 us
    unnamed x13, local copies, waits for them, and re-layouts  4.83 us

profile of v1, /device:TPU:1, one launch (start us, length us, event | category | flops | bytes accessed | tf_op | source)
XLA Modules:
  0.0 82.7 jit_solution(17580506630633297371)
XLA Ops:
  0.0 0.8 copy.9.elec_ref
  0.8 0.8 copy.8
  1.5 0.1 reshape.6
  1.6 0.0 copy-start.4
  1.6 0.7 copy-done.4
  2.3 0.0 copy-start.2
  2.3 0.0 copy-start.3
  2.3 0.1 copy.10.rec_ref
  2.4 0.6 copy-done.2
  3.0 0.0 copy-done.3
  3.0 0.0 copy-start
  3.0 0.9 %copy-done = f32[4,4,32,128]{3,2,1,0:T(8,128)S(1)} copy-done((f32[4,4,32,128]{3,2,1,0:T(8,128)S(1)}, f32[4,4,32,128]{3,2,1,0:T(8,128)}, u32[]{:S(2)}) %copy-start) | copy-done | bytes 262168
  4.0 0.0 copy-start.1
  4.0 0.9 %copy-done.1 = f32[4,4,32,128]{3,2,1,0:T(8,128)S(1)} copy-done((f32[4,4,32,128]{3,2,1,0:T(8,128)S(1)}, f32[4,4,32,128]{3,2,1,0:T(8,128)}, u32[]{:S(2)}) %copy-start.1) | copy-done | bytes 262168
  4.9 77.0 %shard_map.73 = f32[16,128]{1,0:T(8,128)S(1)} custom-call(f32[4,4,32,128]{3,2,1,0:T(8,128)S(1)} %copy-done, f32[4,4,32,128]{3,2,1,0:T(8,128)S(1)} %copy-done.1, f32[16,128]{1,0:T(8,128)S(1)} %bitcast.6, s32[32,2]{1,0:T(8,128)S(1)} %copy.9.elec_ref, s32[128,2]{1,0:T(8,128)S(1)} %copy.10.rec_ref, f32[32,128]{1,0:T(8,128)S(1)} %copy-done.2, s32[32]{0:T(128)S(1)} %copy-done.3), custom_call_target="tpu_custom_call" | custom-call | tf_op jit(solution)/shard_map/pallas_call | solution.py:477
  82.0 0.1 reshape.7
  82.0 0.6 copy.11
Async XLA Ops:
  1.6 0.7 copy-start.4
  2.3 0.7 copy-start.2
  2.3 0.7 copy-start.3
  3.0 1.0 %copy-start = (f32[4,4,32,128]{3,2,1,0:T(8,128)S(1)}, f32[4,4,32,128]{3,2,1,0:T(8,128)}, u32[]{:S(2)}) copy-start(f32[4,4,32,128]{3,2,1,0:T(8,128)} %wp_ref.1) | copy-start | bytes 786436
  4.0 0.9 %copy-start.1 = (f32[4,4,32,128]{3,2,1,0:T(8,128)S(1)}, f32[4,4,32,128]{3,2,1,0:T(8,128)}, u32[]{:S(2)}) copy-start(f32[4,4,32,128]{3,2,1,0:T(8,128)} %wa_ref.1) | copy-start | bytes 786436

commit v2 on v1

--- a/solution.py
+++ b/solution.py
@@ -40,6 +40,7 @@
 
 
 STEPS = chebyshev()
+BLOCKS = {22: 11, 20: 5, 18: 6, 16: 4, 14: 7, 12: 6, 10: 5}
 
 
 def split3(v):
@@ -51,8 +52,9 @@
 
 
 def kernel(
-    wp_ref, wa_ref, cond_ref, elec_ref, rec_ref, obs_ref, order_ref,
+    wp_ref, wa_ref, cond_hbm, elec_hbm, rec_hbm, obs_hbm, order_hbm,
     out_ref,
+    cond_v, cond_ref, elec_ref, rec_v, obs_ref, order_ref,
     p0, p1, a0, a1, cext, coef, slope, gath, pan, pick, pick_own,
     scond, scoef, sinv, srhs, y0, y1, vm, zbuf, gbuf, gt, rbuf,
     loc_sem, warm_s, warm_r, cond_s, cond_r, src_s, src_r, z_s, z_r, g_s, g_r, rs_s, rs_r,
@@ -92,11 +94,23 @@
     half = pl.ds(2 * core, 2)
     own_p = pltpu.make_async_copy(wp_ref.at[half], p0.at[:, own_x, HALO : HALO + YR, :], loc_sem.at[0])
     own_a = pltpu.make_async_copy(wa_ref.at[half], a0.at[:, own_x, HALO : HALO + YR, :], loc_sem.at[1])
+    small = [
+        pltpu.make_async_copy(a, b, loc_sem.at[2 + i])
+        for i, (a, b) in enumerate(
+            ((cond_hbm, cond_v), (rec_hbm, rec_v), (order_hbm, order_ref), (elec_hbm, elec_ref), (obs_hbm, obs_ref))
+        )
+    ]
+    for copy in small:
+        copy.start()
     own_p.start()
     own_a.start()
+    for copy in small:
+        copy.wait()
 
     own_rows = pl.ds(pl.multiple_of(16 * src, 16), 16)
-    gath[own_rows, :] = cond_ref[...]
+    piece = jnp.concatenate([cond_v[x] for x in range(XR)], axis=1)
+    cond_ref[...] = piece
+    gath[own_rows, :] = piece
 
     pl.semaphore_wait(barrier, len(partners))
 
@@ -135,13 +149,17 @@
 
     copies_p = warm_copies(0, wp_ref, p0)
     copies_a = warm_copies(1, wa_ref, a0)
-    for copy in copies_p:
-        copy.start()
-
-    rx0 = rec_ref[:, 0:1] >> 7
-    ry0 = rec_ref[:, 0:1] & (NY - 1)
-    rx1 = rec_ref[:, 1:2] >> 7
-    ry1 = rec_ref[:, 1:2] & (NY - 1)
+    straight = [dz == 0 or dg == 0 for dz, t, dg in halo]
+    for copy, now in zip(copies_p, straight):
+        if now:
+            copy.start()
+
+    cells = jnp.concatenate([rec_v[...].astype(F32), jnp.zeros((126, 128), F32)], axis=0)
+    cells = jnp.transpose(cells).astype(I32)
+    rx0 = cells[:, 0:1] >> 7
+    ry0 = cells[:, 0:1] & (NY - 1)
+    rx1 = cells[:, 1:2] >> 7
+    ry1 = cells[:, 1:2] & (NY - 1)
 
     def own_flat(cx, cy):
         lx = cx - CX * zc
@@ -186,6 +204,9 @@
         )
     for copy in copies_c:
         copy.start()
+    for copy, now in zip(copies_p, straight):
+        if not now:
+            copy.start()
     for copy in copies_a:
         copy.start()
     for copy in copies_c:
@@ -222,7 +243,7 @@
             coef[i, r] = h * inv
         return carry
 
-    lax.fori_loop(1, EX - 1, coef_row, 0)
+    lax.fori_loop(1, EX - 1, coef_row, 0, unroll=2)
 
     def slope_of(s, n):
         total = s + n
@@ -302,7 +323,7 @@
     idents = [order_ref[first_slot + j] for j in range(2)]
     rhs = jnp.zeros(shape, F32)
     for e, sign in ((0, strength), (1, -strength)):
-        cells = [elec_ref[k, e] for k in idents]
+        cells = [elec_ref[e, k] for k in idents]
         ex = jnp.where(lane3 < 64, cells[0] >> 7, cells[1] >> 7)
         ey = jnp.where(lane3 < 64, cells[0] & (NY - 1), cells[1] & (NY - 1))
         hit = (ex == row3) & (ey == y3) & (sub3 == 0) & ((lane3 & 63) < EY)
@@ -310,33 +331,43 @@
     srhs[...] = rhs
     thin_p = thin_solve()
 
-    def full_solve(x0, x1):
-        def app(x, prev, dest, wc, wu, wp, e):
-            def row(r, carry):
+    def app(x, prev, dest, wc, wu, wp, e):
+        rows = CX + 2 * e
+        block = BLOCKS[rows]
+
+        def step(q, carry):
+            fresh = []
+            for i in range(block):
+                r = HALO - e + q * block + i
+                c = [coef[j, r] for j in range(6)]
                 for slot in range(2):
                     u = x[slot, r]
-                    total = coef[0, r] * x[slot, r - 1] + coef[1, r] * x[slot, r + 1]
-                    total = total + coef[2, r] * pltpu.roll(u, 1, 0) + coef[3, r] * pltpu.roll(u, EY - 1, 0)
-                    total = total + coef[4, r] * pltpu.roll(u, 1, 1) + coef[5, r] * pltpu.roll(u, 127, 1)
-                    fresh = wu * u + wc * total
+                    total = c[0] * x[slot, r - 1] + c[1] * x[slot, r + 1]
+                    total = total + c[2] * pltpu.roll(u, 1, 0) + c[3] * pltpu.roll(u, EY - 1, 0)
+                    total = total + c[4] * pltpu.roll(u, 1, 1) + c[5] * pltpu.roll(u, 127, 1)
+                    value = wu * u + wc * total
                     if prev is not None:
-                        fresh = fresh - wp * prev[slot, r]
-                    dest[slot, r] = fresh
-                return carry
-
-            lax.fori_loop(HALO - e, HALO + CX + e, row, 0)
-
-        app(x0, None, x1, 1.0 / centre, 1.0 - 1.0 / centre, 0.0, HALO - 1)
-        older, newer = x0, x1
-        for k, (a, b) in enumerate(STEPS):
-            app(newer, older, older, b, 1.0 + a - b, a, HALO - 2 - k)
-            older, newer = newer, older
-        return newer
+                        value = value - wp * prev[slot, r]
+                    fresh.append((slot, r, value))
+            for slot, r, value in fresh:
+                dest[slot, r] = value
+            return carry
+
+        lax.fori_loop(0, rows // block, step, 0)
+
+    def full_solve(x0, x1, first, last):
+        if first == 0:
+            app(x0, None, x1, 1.0 / centre, 1.0 - 1.0 / centre, 0.0, HALO - 1)
+        for k in range(max(first, 1), last):
+            a, b = STEPS[k - 1]
+            older, newer = (x0, x1) if k % 2 else (x1, x0)
+            app(newer, older, older, b, 1.0 + a - b, a, HALO - 1 - k)
+        return x1
 
     own_p.wait()
     for copy in copies_p:
         copy.wait_recv()
-    pot = full_solve(p0, p1)
+    pot = full_solve(p0, p1, 0, SWEEPS + 1)
     add_thin(thin_p, pot)
 
     value = jnp.zeros((128, 128), F32)
@@ -359,7 +390,10 @@
     for copy in copies_z:
         copy.start()
 
-    lax.fori_loop(HALO, HALO + CX, slope_row, 0)
+    own_a.wait()
+    for copy in copies_a:
+        copy.wait_recv()
+    full_solve(a0, a1, 0, 4)
 
     for copy in copies_z:
         copy.wait_recv()
@@ -377,10 +411,8 @@
     for copy in copies_g:
         copy.start()
 
-    own_a.wait()
-    for copy in copies_a:
-        copy.wait_recv()
-    adj = full_solve(a0, a1)
+    adj = full_solve(a0, a1, 4, SWEEPS + 1)
+    lax.fori_loop(HALO, HALO + CX, slope_row, 0, unroll=2)
 
     for copy in copies_g:
         copy.wait_recv()
@@ -430,10 +462,7 @@
 
     pan8 = slope.at[0, :, 0:YR, :]
 
-    def grad_row_stored(r, carry):
-        return grad_row(r, carry)
-
-    lax.fori_loop(HALO, HALO + CX, grad_row_stored, 0)
+    lax.fori_loop(HALO, HALO + CX, grad_row, 0, unroll=2)
     for c in range(2):
         gt[c] = jnp.transpose(slope[0, XR * c : XR * c + XR, 0:YR, :].reshape(128, 128))
 
@@ -457,7 +486,9 @@
         for t in (0, 1):
             if ds or t:
                 total = total + rbuf[t, ds]
-    out_ref[...] = -total
+    total = -total
+    for x in range(XR):
+        out_ref[x] = (pltpu.roll(total, 128 - YR * x, 1) if x else total)[:, :YR]
 
     for copies in (gathers, copies_p, copies_a, copies_c, copies_z, copies_g, copies_rs):
         for copy in copies:
@@ -466,20 +497,24 @@
 
 def body(warm_potential, warm_adjoint, conductivity, electrodes, receivers, observed, source_order):
     xr, yr, depth = conductivity.shape
-    turned = conductivity.reshape(xr * yr, depth).T
-    anyspace = pl.BlockSpec(memory_space=pl.ANY)
+    hbm = pl.BlockSpec(memory_space=pltpu.HBM)
     vmem = pl.BlockSpec(memory_space=pltpu.VMEM)
-    smem = pl.BlockSpec(memory_space=pltpu.SMEM)
     field = pltpu.VMEM((2, EX, EY, 128), F32)
     thin = pltpu.VMEM((EX, 8, 128), F32)
     inner = pltpu.VMEM((EX - 2, 8, 128), F32)
     dma = pltpu.SemaphoreType.DMA
     result = pl.pallas_call(
         kernel,
-        out_shape=jax.ShapeDtypeStruct((16, 128), F32),
-        in_specs=[anyspace, anyspace, vmem, smem, vmem, vmem, smem],
+        out_shape=jax.ShapeDtypeStruct((xr, depth, yr), F32),
+        in_specs=[hbm] * 7,
         out_specs=vmem,
         scratch_shapes=[
+            pltpu.VMEM((xr, depth, yr), F32),
+            pltpu.VMEM((depth, xr * yr), F32),
+            pltpu.SMEM((2, 32), I32),
+            pltpu.VMEM((2, 128), I32),
+            pltpu.VMEM((32, 128), F32),
+            pltpu.SMEM((32,), I32),
             field, field, field, field,
             pltpu.VMEM((EX, EY, 128), F32),
             pltpu.VMEM((6, EX, EY, 128), F32),
@@ -496,7 +531,7 @@
             pltpu.VMEM((NGY - 1, 8, 128), F32),
             pltpu.VMEM((2, 128, 128), F32),
             pltpu.VMEM((2, NSRCG, 16, 128), F32),
-            dma((2,)),
+            dma((7,)),
             dma((2, 3, 2, 3)), dma((2, 3, 2, 3)),
             dma((3, 2, 3)), dma((3, 2, 3)),
             dma((NSRCG - 1,)), dma((NSRCG - 1,)),
@@ -505,10 +540,13 @@
             dma((2, NSRCG)), dma((2, NSRCG)),
         ],
         compiler_params=pltpu.CompilerParams(
-            collective_id=0, has_side_effects=True, vmem_limit_bytes=40 * 1024 * 1024
+            collective_id=0, has_side_effects=True, vmem_limit_bytes=63 * 1024 * 1024
         ),
-    )(warm_potential, warm_adjoint, turned, electrodes, receivers, observed, source_order)
-    return result.T.reshape(xr, yr, depth)
+    )(
+        warm_potential, warm_adjoint, jnp.transpose(conductivity, (0, 2, 1)), electrodes.T, receivers.T,
+        observed, source_order,
+    )
+    return jnp.transpose(result, (0, 2, 1))
 
 
 def solution(mesh):

time: 83 us -> 62.1 us (0.75)
  Pallas kernels: 77 us -> 60.5 us
  local copies, waits for them, and re-layouts: 5.61 us -> 1.38 us
    pallas_call x1, Pallas kernels: 77 us -> 60.5 us  [body(): pl.pallas_call(kernel, out_shape=jax.ShapeDtypeStruct((xr, depth, yr), F3...]
    unnamed x13 -> x1, local copies, waits for them, and re-layouts: 4.83 us -> 1.38 us
where the time goes in v2:
time: 62.1 us; the launch traced here: 61.9 us
  Pallas kernels  60.5 us (97%)
  local copies, waits for them, and re-layouts  1.38 us (2%)
    pallas_call x1, Pallas kernels, body(): pl.pallas_call(kernel, out_shape=jax.ShapeDtypeStruct((xr, depth, yr), F3...  60.5 us
    unnamed x1, local copies, waits for them, and re-layouts  1.38 us

profile of v2, /device:TPU:1, one launch (start us, length us, event | category | flops | bytes accessed | tf_op | source)
XLA Modules:
  0.0 61.9 jit_solution(10632045244097277014)
XLA Ops:
  0.0 60.5 %shard_map.73 = f32[4,16,32]{2,1,0:T(8,128)} custom-call(f32[4,4,32,128]{3,2,1,0:T(8,128)} %wp_ref.1, f32[4,4,32,128]{3,2,1,0:T(8,128)} %wa_ref.1, f32[4,16,32]{2,1,0:T(8,128)} %bitcast.5, s32[2,32]{1,0:T(2,128)} %bitcast.6, s32[2,128]{1,0:T(2,128)} %bitcast.7, f32[32,128]{1,0:T(8,128)} %obs_hbm.1, s32[32]{0:T(128)} %order_hbm.1), custom_call_target="tpu_custom_call" | custom-call | tf_op jit(solution)/shard_map/pallas_call | solution.py:506
  60.5 1.4 %copy.9 = f32[4,32,16]{1,2,0:T(8,128)} copy(f32[4,32,16]{1,2,0:T(8,128)} %bitcast.4) | data formatting | bytes 16384

commit v3 on v2

--- a/solution.py
+++ b/solution.py
@@ -40,7 +40,7 @@
 
 
 STEPS = chebyshev()
-BLOCKS = {22: 11, 20: 5, 18: 6, 16: 4, 14: 7, 12: 6, 10: 5}
+BLOCKS = {22: 11, 20: 10, 18: 9, 16: 8, 14: 7, 12: 12, 10: 10}
 
 
 def split3(v):
@@ -91,32 +91,39 @@
         pl.semaphore_signal(barrier, inc=1, device_id=device, device_id_type=MESH)
 
     own_x = pl.ds(HALO + XR * core, XR)
-    half = pl.ds(2 * core, 2)
-    own_p = pltpu.make_async_copy(wp_ref.at[half], p0.at[:, own_x, HALO : HALO + YR, :], loc_sem.at[0])
-    own_a = pltpu.make_async_copy(wa_ref.at[half], a0.at[:, own_x, HALO : HALO + YR, :], loc_sem.at[1])
+    def settle(ref, sem):
+        pltpu.make_async_copy(ref, ref, sem).wait()
+
+    owns = [
+        pltpu.make_async_copy(
+            ref.at[2 * core + slot], dest.at[slot, own_x, HALO : HALO + YR, :], warm_r.at[which, slot]
+        )
+        for which, (ref, dest) in enumerate(((wp_ref, p0), (wa_ref, a0)))
+        for slot in range(2)
+    ]
     small = [
-        pltpu.make_async_copy(a, b, loc_sem.at[2 + i])
+        pltpu.make_async_copy(a, b, loc_sem.at[i])
         for i, (a, b) in enumerate(
             ((cond_hbm, cond_v), (rec_hbm, rec_v), (order_hbm, order_ref), (elec_hbm, elec_ref), (obs_hbm, obs_ref))
         )
     ]
     for copy in small:
         copy.start()
-    own_p.start()
-    own_a.start()
+    for copy in owns:
+        copy.start()
     for copy in small:
         copy.wait()
 
     own_rows = pl.ds(pl.multiple_of(16 * src, 16), 16)
     piece = jnp.concatenate([cond_v[x] for x in range(XR)], axis=1)
     cond_ref[...] = piece
-    gath[own_rows, :] = piece
+    pltpu.make_async_copy(cond_ref, gath.at[own_rows, :], src_r).start()
 
     pl.semaphore_wait(barrier, len(partners))
 
     gathers = [
         pltpu.make_async_remote_copy(
-            cond_ref, gath.at[own_rows, :], src_s.at[ds - 1], src_r.at[ds - 1],
+            cond_ref, gath.at[own_rows, :], src_s, src_r,
             device_id=place(ds=ds), device_id_type=MESH,
         )
         for ds in range(1, NSRCG)
@@ -131,28 +138,25 @@
             return slice(YR - HALO, YR), slice(0, HALO)
         return slice(0, HALO), slice(HALO + YR, EY)
 
-    def warm_copies(which, ref, dest):
+    def warm_copies(which, ref, dest, slot):
         copies = []
         for dz, t, dg in halo:
             ys, yd = y_spans(dg)
             c2 = core if t == 0 else 1 - core
             copies.append(
                 pltpu.make_async_remote_copy(
-                    ref.at[pl.ds(2 * c2, 2), :, ys, :],
-                    dest.at[:, pl.ds(HALO * (1 - dz) + XR * core, XR), yd, :],
-                    warm_s.at[which, dz + 1, t, dg + 1],
-                    warm_r.at[which, dz + 1, t, dg + 1],
+                    ref.at[2 * c2 + slot, :, ys, :],
+                    dest.at[slot, pl.ds(HALO * (1 - dz) + XR * core, XR), yd, :],
+                    warm_s.at[which, slot], warm_r.at[which, slot],
                     device_id=place(dz=dz, t=t, dg=dg), device_id_type=MESH,
                 )
             )
         return copies
 
-    copies_p = warm_copies(0, wp_ref, p0)
-    copies_a = warm_copies(1, wa_ref, a0)
-    straight = [dz == 0 or dg == 0 for dz, t, dg in halo]
-    for copy, now in zip(copies_p, straight):
-        if now:
-            copy.start()
+    copies_p = [warm_copies(0, wp_ref, p0, slot) for slot in range(2)]
+    copies_a = [warm_copies(1, wa_ref, a0, slot) for slot in range(2)]
+    for copy in copies_p[0]:
+        copy.start()
 
     cells = jnp.concatenate([rec_v[...].astype(F32), jnp.zeros((126, 128), F32)], axis=0)
     cells = jnp.transpose(cells).astype(I32)
@@ -186,10 +190,9 @@
             jnp.where(col0 == xrow, 1.0, 0.0) - jnp.where(col1 == xrow, 1.0, 0.0)
         ).astype(BF16)
 
-    for copy in gathers:
-        copy.wait_recv()
+    settle(gath, src_r)
     pan[...] = jnp.transpose(gath[...]).reshape(XR, YR, 128)
-    cext[own_x, HALO : HALO + YR, :] = pan[...]
+    pltpu.make_async_copy(pan, cext.at[own_x, HALO : HALO + YR, :], cond_r).start()
     copies_c = []
     for dz, t, dg in halo:
         ys, yd = y_spans(dg)
@@ -197,20 +200,17 @@
             pltpu.make_async_remote_copy(
                 pan.at[:, ys, :],
                 cext.at[pl.ds(HALO * (1 - dz) + XR * core, XR), yd, :],
-                cond_s.at[dz + 1, t, dg + 1],
-                cond_r.at[dz + 1, t, dg + 1],
+                cond_s, cond_r,
                 device_id=place(dz=dz, t=t, dg=dg), device_id_type=MESH,
             )
         )
     for copy in copies_c:
         copy.start()
-    for copy, now in zip(copies_p, straight):
-        if not now:
-            copy.start()
-    for copy in copies_a:
-        copy.start()
-    for copy in copies_c:
-        copy.wait_recv()
+    for copy in copies_p[1]:
+        copy.start()
+    settle(cext, cond_r)
+    for copy in copies_a[0]:
+        copy.start()
 
     yy = (YR * gy - HALO + lax.broadcasted_iota(I32, (EY, 128), 0)) & (NY - 1)
     zz = lax.broadcasted_iota(I32, (EY, 128), 1)
@@ -260,6 +260,38 @@
         slope[4, q] = jnp.where(in_zm, slope_of(s, pltpu.roll(s, 1, 1)), 0.0)
         slope[5, q] = jnp.where(in_zp, slope_of(s, pltpu.roll(s, 127, 1)), 1.0)
         return carry
+
+    def app(slot, x, prev, dest, wc, wu, wp, e):
+        rows = CX + 2 * e
+        block = BLOCKS[rows]
+
+        def step(q, carry):
+            fresh = []
+            for i in range(block):
+                r = HALO - e + q * block + i
+                u = x[slot, r]
+                total = coef[0, r] * x[slot, r - 1] + coef[1, r] * x[slot, r + 1]
+                total = total + coef[2, r] * pltpu.roll(u, 1, 0) + coef[3, r] * pltpu.roll(u, EY - 1, 0)
+                total = total + coef[4, r] * pltpu.roll(u, 1, 1) + coef[5, r] * pltpu.roll(u, 127, 1)
+                value = wu * u + wc * total
+                if prev is not None:
+                    value = value - wp * prev[slot, r]
+                fresh.append((r, value))
+            for r, value in fresh:
+                dest[slot, r] = value
+            return carry
+
+        lax.fori_loop(0, rows // block, step, 0)
+
+    def full_solve(which, slot, x0, x1):
+        settle(x0.at[slot], warm_r.at[which, slot])
+        app(slot, x0, None, x1, 1.0 / centre, 1.0 - 1.0 / centre, 0.0, HALO - 1)
+        for k, (a, b) in enumerate(STEPS):
+            older, newer = (x1, x0) if k % 2 else (x0, x1)
+            app(slot, newer, older, older, b, 1.0 + a - b, a, HALO - 2 - k)
+
+    pot, adj = p1, a1
+    full_solve(0, 0, p0, p1)
 
     for first, count in ((0, 16), (16, 8)):
         gathered = jnp.ones((EY, 128), F32)
@@ -331,43 +363,9 @@
     srhs[...] = rhs
     thin_p = thin_solve()
 
-    def app(x, prev, dest, wc, wu, wp, e):
-        rows = CX + 2 * e
-        block = BLOCKS[rows]
-
-        def step(q, carry):
-            fresh = []
-            for i in range(block):
-                r = HALO - e + q * block + i
-                c = [coef[j, r] for j in range(6)]
-                for slot in range(2):
-                    u = x[slot, r]
-                    total = c[0] * x[slot, r - 1] + c[1] * x[slot, r + 1]
-                    total = total + c[2] * pltpu.roll(u, 1, 0) + c[3] * pltpu.roll(u, EY - 1, 0)
-                    total = total + c[4] * pltpu.roll(u, 1, 1) + c[5] * pltpu.roll(u, 127, 1)
-                    value = wu * u + wc * total
-                    if prev is not None:
-                        value = value - wp * prev[slot, r]
-                    fresh.append((slot, r, value))
-            for slot, r, value in fresh:
-                dest[slot, r] = value
-            return carry
-
-        lax.fori_loop(0, rows // block, step, 0)
-
-    def full_solve(x0, x1, first, last):
-        if first == 0:
-            app(x0, None, x1, 1.0 / centre, 1.0 - 1.0 / centre, 0.0, HALO - 1)
-        for k in range(max(first, 1), last):
-            a, b = STEPS[k - 1]
-            older, newer = (x0, x1) if k % 2 else (x1, x0)
-            app(newer, older, older, b, 1.0 + a - b, a, HALO - 1 - k)
-        return x1
-
-    own_p.wait()
-    for copy in copies_p:
-        copy.wait_recv()
-    pot = full_solve(p0, p1, 0, SWEEPS + 1)
+    for copy in copies_a[1]:
+        copy.start()
+    full_solve(0, 1, p0, p1)
     add_thin(thin_p, pot)
 
     value = jnp.zeros((128, 128), F32)
@@ -382,7 +380,7 @@
     vm[0] = jnp.transpose(value)[0:8]
     copies_z = [
         pltpu.make_async_remote_copy(
-            vm.at[0], zbuf.at[dz - 1], z_s.at[dz - 1], z_r.at[dz - 1],
+            vm.at[0], zbuf.at[dz - 1], z_s, z_r,
             device_id=place(dz=dz), device_id_type=MESH,
         )
         for dz in range(1, NZC)
@@ -390,20 +388,17 @@
     for copy in copies_z:
         copy.start()
 
-    own_a.wait()
-    for copy in copies_a:
-        copy.wait_recv()
-    full_solve(a0, a1, 0, 4)
-
-    for copy in copies_z:
-        copy.wait_recv()
+    lax.fori_loop(HALO, HALO + CX, slope_row, 0, unroll=2)
+    full_solve(1, 0, a0, a1)
+
+    settle(zbuf, z_r)
     total = vm[0]
     for i in range(NZC - 1):
         total = total + zbuf[i]
     vm[1] = total
     copies_g = [
         pltpu.make_async_remote_copy(
-            vm.at[1], gbuf.at[dg - 1], g_s.at[dg - 1], g_r.at[dg - 1],
+            vm.at[1], gbuf.at[dg - 1], g_s, g_r,
             device_id=place(dg=dg), device_id_type=MESH,
         )
         for dg in range(1, NGY)
@@ -411,11 +406,10 @@
     for copy in copies_g:
         copy.start()
 
-    adj = full_solve(a0, a1, 4, SWEEPS + 1)
-    lax.fori_loop(HALO, HALO + CX, slope_row, 0, unroll=2)
-
-    for copy in copies_g:
-        copy.wait_recv()
+    full_solve(1, 1, a0, a1)
+
+
+    settle(gbuf, g_r)
     total = vm[1]
     for i in range(NGY - 1):
         total = total + gbuf[i]
@@ -472,27 +466,31 @@
         return pltpu.make_async_remote_copy(
             gt.at[c2, pl.ds(pl.multiple_of(16 * s2, 16), 16), :],
             rbuf.at[t, ds],
-            rs_s.at[t, ds], rs_r.at[t, ds],
+            rs_s, rs_r,
             device_id=place(ds=ds, t=t), device_id_type=MESH,
         )
 
     copies_rs = [rs_copy(ds, t) for ds in range(NSRCG) for t in (0, 1) if ds or t]
     for copy in copies_rs:
         copy.start()
-    for copy in copies_rs:
-        copy.wait_recv()
-    total = gt[core, own_rows, :]
-    for ds in range(NSRCG):
-        for t in (0, 1):
-            if ds or t:
-                total = total + rbuf[t, ds]
+    pltpu.make_async_copy(gt.at[core, own_rows, :], rbuf.at[0, 0], rs_r).start()
+    settle(rbuf, rs_r)
+    total = rbuf[0, 0] + rbuf[1, 0]
+    for ds in range(1, NSRCG):
+        total = total + (rbuf[0, ds] + rbuf[1, ds])
     total = -total
     for x in range(XR):
         out_ref[x] = (pltpu.roll(total, 128 - YR * x, 1) if x else total)[:, :YR]
 
-    for copies in (gathers, copies_p, copies_a, copies_c, copies_z, copies_g, copies_rs):
-        for copy in copies:
-            copy.wait_send()
+    sent = p0.at[:, 0:16, 0:YR, :]
+    for which in range(2):
+        for slot in range(2):
+            settle(sent, warm_s.at[which, slot])
+    settle(sent, cond_s)
+    settle(gath.at[0 : 16 * (NSRCG - 1), :], src_s)
+    settle(zbuf, z_s)
+    settle(gbuf, g_s)
+    settle(gt.at[:, 0 : 8 * (2 * NSRCG - 1), :], rs_s)
 
 
 def body(warm_potential, warm_adjoint, conductivity, electrodes, receivers, observed, source_order):
@@ -531,13 +529,9 @@
             pltpu.VMEM((NGY - 1, 8, 128), F32),
             pltpu.VMEM((2, 128, 128), F32),
             pltpu.VMEM((2, NSRCG, 16, 128), F32),
-            dma((7,)),
-            dma((2, 3, 2, 3)), dma((2, 3, 2, 3)),
-            dma((3, 2, 3)), dma((3, 2, 3)),
-            dma((NSRCG - 1,)), dma((NSRCG - 1,)),
-            dma((NZC - 1,)), dma((NZC - 1,)),
-            dma((NGY - 1,)), dma((NGY - 1,)),
-            dma((2, NSRCG)), dma((2, NSRCG)),
+            dma((5,)),
+            dma((2, 2)), dma((2, 2)),
+            *([dma] * 10),
         ],
         compiler_params=pltpu.CompilerParams(
             collective_id=0, has_side_effects=True, vmem_limit_bytes=63 * 1024 * 1024

time: 62.1 us -> 58.5 us (0.942)
  Pallas kernels: 60.5 us -> 56.9 us
    pallas_call x1, Pallas kernels: 60.5 us -> 56.9 us  [body(): pl.pallas_call(kernel, out_shape=jax.ShapeDtypeStruct((xr, depth, yr), F3...]
where the time goes in v3:
time: 58.5 us; the launch traced here: 58.3 us
  Pallas kernels  56.9 us (97%)
  local copies, waits for them, and re-layouts  1.38 us (2%)
    pallas_call x1, Pallas kernels, body(): pl.pallas_call(kernel, out_shape=jax.ShapeDtypeStruct((xr, depth, yr), F3...  56.9 us
    unnamed x1, local copies, waits for them, and re-layouts  1.38 us

profile of v3, /device:TPU:1, one launch (start us, length us, event | category | flops | bytes accessed | tf_op | source)
XLA Modules:
  0.0 58.3 jit_solution(670855769093907301)
XLA Ops:
  0.0 56.9 %shard_map.73 = f32[4,16,32]{2,1,0:T(8,128)} custom-call(f32[4,4,32,128]{3,2,1,0:T(8,128)} %wp_ref.1, f32[4,4,32,128]{3,2,1,0:T(8,128)} %wa_ref.1, f32[4,16,32]{2,1,0:T(8,128)} %bitcast.5, s32[2,32]{1,0:T(2,128)} %bitcast.6, s32[2,128]{1,0:T(2,128)} %bitcast.7, f32[32,128]{1,0:T(8,128)} %obs_hbm.1, s32[32]{0:T(128)} %order_hbm.1), custom_call_target="tpu_custom_call" | custom-call | tf_op jit(solution)/shard_map/pallas_call | solution.py:504
  56.9 1.4 %copy.9 = f32[4,32,16]{1,2,0:T(8,128)} copy(f32[4,32,16]{1,2,0:T(8,128)} %bitcast.4) | data formatting | bytes 16384

commit v4 on v3

--- a/solution.py
+++ b/solution.py
@@ -55,8 +55,10 @@
     wp_ref, wa_ref, cond_hbm, elec_hbm, rec_hbm, obs_hbm, order_hbm,
     out_ref,
     cond_v, cond_ref, elec_ref, rec_v, obs_ref, order_ref,
-    p0, p1, a0, a1, cext, coef, slope, gath, pan, pick, pick_own,
+    p0, p1, a0, a1, cext, coef, slope, gath, pan, pick,
+    wp_v, flat_p, edge_p, thin_main, thin_edge,
     scond, scoef, sinv, srhs, y0, y1, vm, zbuf, gbuf, gt, rbuf,
+    main_s, main_r, edge_s, edge_r,
     loc_sem, warm_s, warm_r, cond_s, cond_r, src_s, src_r, z_s, z_r, g_s, g_r, rs_s, rs_r,
 ):
     src = lax.axis_index("src")
@@ -104,7 +106,10 @@
     small = [
         pltpu.make_async_copy(a, b, loc_sem.at[i])
         for i, (a, b) in enumerate(
-            ((cond_hbm, cond_v), (rec_hbm, rec_v), (order_hbm, order_ref), (elec_hbm, elec_ref), (obs_hbm, obs_ref))
+            (
+                (cond_hbm, cond_v), (rec_hbm, rec_v), (order_hbm, order_ref), (elec_hbm, elec_ref),
+                (obs_hbm, obs_ref), (wp_ref, wp_v),
+            )
         )
     ]
     for copy in small:
@@ -118,6 +123,12 @@
     piece = jnp.concatenate([cond_v[x] for x in range(XR)], axis=1)
     cond_ref[...] = piece
     pltpu.make_async_copy(cond_ref, gath.at[own_rows, :], src_r).start()
+
+    for x in range(XR):
+        flat_p[x] = jnp.transpose(wp_v[:, x].reshape(128, 128))[0:8]
+    for side, ys in enumerate((slice(YR - HALO, YR), slice(0, HALO))):
+        edge_p[side] = jnp.transpose(wp_v[:, :, ys, :].reshape(128, 128))[0:8]
+    pltpu.make_async_copy(flat_p, thin_main.at[own_x], main_r).start()
 
     pl.semaphore_wait(barrier, len(partners))
 
@@ -155,6 +166,17 @@
 
     copies_p = [warm_copies(0, wp_ref, p0, slot) for slot in range(2)]
     copies_a = [warm_copies(1, wa_ref, a0, slot) for slot in range(2)]
+    for dz, t, dg in halo:
+        if dg == 0:
+            a, b = flat_p, thin_main.at[pl.ds(HALO * (1 - dz) + XR * core, XR)]
+            sems = main_s, main_r
+        else:
+            side = 0 if dg == 1 else 1
+            a, b = edge_p.at[side], thin_edge.at[side, 2 * (1 - dz) + core]
+            sems = edge_s, edge_r
+        pltpu.make_async_remote_copy(
+            a, b, *sems, device_id=place(dz=dz, t=t, dg=dg), device_id_type=MESH
+        ).start()
     for copy in copies_p[0]:
         copy.start()
 
@@ -164,18 +186,6 @@
     ry0 = cells[:, 0:1] & (NY - 1)
     rx1 = cells[:, 1:2] >> 7
     ry1 = cells[:, 1:2] & (NY - 1)
-
-    def own_flat(cx, cy):
-        lx = cx - CX * zc
-        ly = cy - YR * gy
-        inside = (lx >= 0) & (lx < CX) & (ly >= 0) & (ly < YR)
-        return jnp.where(inside, lx * YR + ly, -1)
-
-    flats = lax.broadcasted_iota(I32, (128, CX * YR), 1)
-    pick_own[...] = (
-        jnp.where(own_flat(rx0, ry0) == flats, 1.0, 0.0)
-        - jnp.where(own_flat(rx1, ry1) == flats, 1.0, 0.0)
-    ).astype(BF16)
 
     lanes = lax.broadcasted_iota(I32, (128, 128), 1)
     ylane = lanes & 63
@@ -209,8 +219,6 @@
     for copy in copies_p[1]:
         copy.start()
     settle(cext, cond_r)
-    for copy in copies_a[0]:
-        copy.start()
 
     yy = (YR * gy - HALO + lax.broadcasted_iota(I32, (EY, 128), 0)) & (NY - 1)
     zz = lax.broadcasted_iota(I32, (EY, 128), 1)
@@ -225,73 +233,6 @@
 
     def harmonic(s, n):
         return 2.0 * s * n / (s + n)
-
-    def coef_row(r, carry):
-        s = cext[r]
-        fm, fp = x_inside(r)
-        hxm = harmonic(s, cext[r - 1]) * fm
-        hxp = harmonic(s, cext[r + 1]) * fp
-        hym = jnp.where(in_ym, harmonic(s, pltpu.roll(s, 1, 0)), 0.0)
-        hyp = jnp.where(in_yp, harmonic(s, pltpu.roll(s, EY - 1, 0)), 0.0)
-        hzm = jnp.where(in_zm, harmonic(s, pltpu.roll(s, 1, 1)), 0.0)
-        hzp = jnp.where(in_zp, harmonic(s, pltpu.roll(s, 127, 1)), 0.0)
-        diag = hxm + hxp + hym + hyp + hzm + hzp
-        diag = diag + s * ((1.0 - fm) + (1.0 - fp))
-        diag = diag + jnp.where(in_ym, 0.0, s) + jnp.where(in_yp, 0.0, s) + jnp.where(in_zp, 0.0, s)
-        inv = 1.0 / diag
-        for i, h in enumerate((hxm, hxp, hym, hyp, hzm, hzp)):
-            coef[i, r] = h * inv
-        return carry
-
-    lax.fori_loop(1, EX - 1, coef_row, 0, unroll=2)
-
-    def slope_of(s, n):
-        total = s + n
-        return 2.0 * n * n / (total * total)
-
-    def slope_row(r, carry):
-        s = cext[r]
-        fm, fp = x_inside(r)
-        q = r - HALO
-        slope[0, q] = slope_of(s, cext[r - 1]) * fm + (1.0 - fm)
-        slope[1, q] = slope_of(s, cext[r + 1]) * fp + (1.0 - fp)
-        slope[2, q] = jnp.where(in_ym, slope_of(s, pltpu.roll(s, 1, 0)), 1.0)
-        slope[3, q] = jnp.where(in_yp, slope_of(s, pltpu.roll(s, EY - 1, 0)), 1.0)
-        slope[4, q] = jnp.where(in_zm, slope_of(s, pltpu.roll(s, 1, 1)), 0.0)
-        slope[5, q] = jnp.where(in_zp, slope_of(s, pltpu.roll(s, 127, 1)), 1.0)
-        return carry
-
-    def app(slot, x, prev, dest, wc, wu, wp, e):
-        rows = CX + 2 * e
-        block = BLOCKS[rows]
-
-        def step(q, carry):
-            fresh = []
-            for i in range(block):
-                r = HALO - e + q * block + i
-                u = x[slot, r]
-                total = coef[0, r] * x[slot, r - 1] + coef[1, r] * x[slot, r + 1]
-                total = total + coef[2, r] * pltpu.roll(u, 1, 0) + coef[3, r] * pltpu.roll(u, EY - 1, 0)
-                total = total + coef[4, r] * pltpu.roll(u, 1, 1) + coef[5, r] * pltpu.roll(u, 127, 1)
-                value = wu * u + wc * total
-                if prev is not None:
-                    value = value - wp * prev[slot, r]
-                fresh.append((r, value))
-            for r, value in fresh:
-                dest[slot, r] = value
-            return carry
-
-        lax.fori_loop(0, rows // block, step, 0)
-
-    def full_solve(which, slot, x0, x1):
-        settle(x0.at[slot], warm_r.at[which, slot])
-        app(slot, x0, None, x1, 1.0 / centre, 1.0 - 1.0 / centre, 0.0, HALO - 1)
-        for k, (a, b) in enumerate(STEPS):
-            older, newer = (x1, x0) if k % 2 else (x0, x1)
-            app(slot, newer, older, older, b, 1.0 + a - b, a, HALO - 2 - k)
-
-    pot, adj = p1, a1
-    full_solve(0, 0, p0, p1)
 
     for first, count in ((0, 16), (16, 8)):
         gathered = jnp.ones((EY, 128), F32)
@@ -324,21 +265,28 @@
     for i, (h, inside, outer) in enumerate(hs):
         scoef[i] = jnp.where(inside, h, 0.0) * inv
 
-    def thin_solve():
-        g = sinv[...] * srhs[...]
+    def thin_apply(x):
+        u = x[1 : EX - 1]
+        total = scoef[0] * x[0 : EX - 2] + scoef[1] * x[2:EX]
+        total = total + scoef[2] * pltpu.roll(u, 1, 2) + scoef[3] * pltpu.roll(u, 127, 2)
+        total = total + scoef[4] * pltpu.roll(u, 1, 1) + scoef[5] * pltpu.roll(u, 7, 1)
+        return u, sinv[...] * srhs[...] + total
+
+    def thin_solve(started):
         zero = jnp.zeros((1, 8, 128), F32)
-        for ref in (y0, y1):
+        for ref in (y1,) if started else (y0, y1):
             ref[0:1] = zero
             ref[EX - 1 : EX] = zero
-        y0[1 : EX - 1] = jnp.zeros(shape, F32)
-        y1[1 : EX - 1] = g * (1.0 / centre)
+        if started:
+            u, total = thin_apply(y0)
+            y1[1 : EX - 1] = (1.0 - 1.0 / centre) * u + (1.0 / centre) * total
+        else:
+            y0[1 : EX - 1] = jnp.zeros(shape, F32)
+            y1[1 : EX - 1] = sinv[...] * srhs[...] * (1.0 / centre)
         older, newer = y0, y1
         for a, b in STEPS:
-            u = newer[1 : EX - 1]
-            total = scoef[0] * newer[0 : EX - 2] + scoef[1] * newer[2:EX]
-            total = total + scoef[2] * pltpu.roll(u, 1, 2) + scoef[3] * pltpu.roll(u, 127, 2)
-            total = total + scoef[4] * pltpu.roll(u, 1, 1) + scoef[5] * pltpu.roll(u, 7, 1)
-            older[1 : EX - 1] = (1.0 + a - b) * u - a * older[1 : EX - 1] + b * (sinv[...] * srhs[...] + total)
+            u, total = thin_apply(newer)
+            older[1 : EX - 1] = (1.0 + a - b) * u - a * older[1 : EX - 1] + b * total
             older, newer = newer, older
         return newer
 
@@ -361,23 +309,45 @@
         hit = (ex == row3) & (ey == y3) & (sub3 == 0) & ((lane3 & 63) < EY)
         rhs = rhs + jnp.where(hit, sign, 0.0)
     srhs[...] = rhs
-    thin_p = thin_solve()
-
-    for copy in copies_a[1]:
-        copy.start()
-    full_solve(0, 1, p0, p1)
-    add_thin(thin_p, pot)
-
-    value = jnp.zeros((128, 128), F32)
-    for slot in range(2):
-        block = pot[slot, HALO : HALO + CX, HALO : HALO + YR, :].reshape(CX * YR, 128)
-        got = jnp.zeros((128, 128), F32)
-        for part in split3(block):
-            got = got + jnp.dot(pick_own[...], part, preferred_element_type=F32)
-        if slot:
-            got = pltpu.roll(got, slot, 1)
-        value = jnp.where(lanes == slot, got, value)
-    vm[0] = jnp.transpose(value)[0:8]
+
+    settle(thin_main, main_r)
+    settle(thin_edge, edge_r)
+    lane1 = lax.broadcasted_iota(I32, (8, 128), 1)
+    ylane1 = lane1 & 63
+
+    def mine(block):
+        return jnp.where(core == 0, block, pltpu.roll(block, 64, 1))
+
+    for r in range(EX):
+        row = mine(thin_main[r])
+        low = mine(thin_edge[0, r // XR])
+        high = mine(thin_edge[1, r // XR])
+        start = jnp.zeros((8, 128), F32)
+        for j in range(2):
+            own_lane = (lane1 >> 6) == j
+            for block, first, at, width in (
+                (row, 32 * j, HALO, YR),
+                (low, 32 * j + 8 * (r % XR), 0, HALO),
+                (high, 32 * j + 8 * (r % XR), HALO + YR, HALO),
+            ):
+                shift = (64 * j + at - first) % 128
+                moved = pltpu.roll(block, shift, 1) if shift else block
+                start = jnp.where(own_lane & (ylane1 >= at) & (ylane1 < at + width), moved, start)
+        y0[r] = start
+    seen_p = thin_solve(True)
+    sub1 = lax.broadcasted_iota(I32, (8, 128), 0)
+    keep = (sub1 == (lane1 >> 6)) & (ylane1 >= HALO) & (ylane1 < HALO + YR)
+    top = jnp.concatenate(
+        [jnp.where(keep, jnp.broadcast_to(seen_p[HALO + i][0:1], (8, 128)), 0.0) for i in range(CX)], axis=1
+    )
+    hi, mid, lo = split3(top)
+    stacked = jnp.concatenate(
+        [hi.astype(F32), mid.astype(F32), lo.astype(F32), jnp.zeros((8, CX * 128), F32)], axis=0
+    ).astype(BF16)
+    got = lax.dot_general(
+        stacked, pick[:, HALO * 128 : (HALO + CX) * 128], (((1,), (1,)), ((), ())), preferred_element_type=F32
+    )
+    vm[0] = got[0:8] + got[8:16] + got[16:24]
     copies_z = [
         pltpu.make_async_remote_copy(
             vm.at[0], zbuf.at[dz - 1], z_s, z_r,
@@ -387,9 +357,77 @@
     ]
     for copy in copies_z:
         copy.start()
-
-    lax.fori_loop(HALO, HALO + CX, slope_row, 0, unroll=2)
-    full_solve(1, 0, a0, a1)
+    thin_p = thin_solve(False)
+    for copy in copies_a[0]:
+        copy.start()
+
+
+    def coef_row(r, carry):
+        s = cext[r]
+        fm, fp = x_inside(r)
+        hxm = harmonic(s, cext[r - 1]) * fm
+        hxp = harmonic(s, cext[r + 1]) * fp
+        hym = jnp.where(in_ym, harmonic(s, pltpu.roll(s, 1, 0)), 0.0)
+        hyp = jnp.where(in_yp, harmonic(s, pltpu.roll(s, EY - 1, 0)), 0.0)
+        hzm = jnp.where(in_zm, harmonic(s, pltpu.roll(s, 1, 1)), 0.0)
+        hzp = jnp.where(in_zp, harmonic(s, pltpu.roll(s, 127, 1)), 0.0)
+        diag = hxm + hxp + hym + hyp + hzm + hzp
+        diag = diag + s * ((1.0 - fm) + (1.0 - fp))
+        diag = diag + jnp.where(in_ym, 0.0, s) + jnp.where(in_yp, 0.0, s) + jnp.where(in_zp, 0.0, s)
+        inv = 1.0 / diag
+        for i, h in enumerate((hxm, hxp, hym, hyp, hzm, hzp)):
+            coef[i, r] = h * inv
+        return carry
+
+    lax.fori_loop(1, EX - 1, coef_row, 0, unroll=2)
+
+    def slope_of(s, n):
+        total = s + n
+        return 2.0 * n * n / (total * total)
+
+    def slope_row(r, carry):
+        s = cext[r]
+        fm, fp = x_inside(r)
+        q = r - HALO
+        slope[0, q] = slope_of(s, cext[r - 1]) * fm + (1.0 - fm)
+        slope[1, q] = slope_of(s, cext[r + 1]) * fp + (1.0 - fp)
+        slope[2, q] = jnp.where(in_ym, slope_of(s, pltpu.roll(s, 1, 0)), 1.0)
+        slope[3, q] = jnp.where(in_yp, slope_of(s, pltpu.roll(s, EY - 1, 0)), 1.0)
+        slope[4, q] = jnp.where(in_zm, slope_of(s, pltpu.roll(s, 1, 1)), 0.0)
+        slope[5, q] = jnp.where(in_zp, slope_of(s, pltpu.roll(s, 127, 1)), 1.0)
+        return carry
+
+    def app(slot, x, prev, dest, wc, wu, wp, e):
+        rows = CX + 2 * e
+        block = BLOCKS[rows]
+
+        def step(q, carry):
+            fresh = []
+            for i in range(block):
+                r = HALO - e + q * block + i
+                u = x[slot, r]
+                total = coef[0, r] * x[slot, r - 1] + coef[1, r] * x[slot, r + 1]
+                total = total + coef[2, r] * pltpu.roll(u, 1, 0) + coef[3, r] * pltpu.roll(u, EY - 1, 0)
+                total = total + coef[4, r] * pltpu.roll(u, 1, 1) + coef[5, r] * pltpu.roll(u, 127, 1)
+                value = wu * u + wc * total
+                if prev is not None:
+                    value = value - wp * prev[slot, r]
+                fresh.append((r, value))
+            for r, value in fresh:
+                dest[slot, r] = value
+            return carry
+
+        lax.fori_loop(0, rows // block, step, 0)
+
+    def full_solve(which, slot, x0, x1):
+        settle(x0.at[slot], warm_r.at[which, slot])
+        app(slot, x0, None, x1, 1.0 / centre, 1.0 - 1.0 / centre, 0.0, HALO - 1)
+        for k, (a, b) in enumerate(STEPS):
+            older, newer = (x1, x0) if k % 2 else (x0, x1)
+            app(slot, newer, older, older, b, 1.0 + a - b, a, HALO - 2 - k)
+
+    pot, adj = p1, a1
+    full_solve(0, 0, p0, p1)
 
     settle(zbuf, z_r)
     total = vm[0]
@@ -405,10 +443,16 @@
     ]
     for copy in copies_g:
         copy.start()
+    for copy in copies_a[1]:
+        copy.start()
+    full_solve(0, 1, p0, p1)
+    add_thin(thin_p, pot)
+
+    lax.fori_loop(HALO, HALO + CX, slope_row, 0, unroll=2)
+    full_solve(1, 0, a0, a1)
+
 
     full_solve(1, 1, a0, a1)
-
-
     settle(gbuf, g_r)
     total = vm[1]
     for i in range(NGY - 1):
@@ -427,7 +471,8 @@
         both = cut[0:8] + cut[8:16] + cut[16:24]
         line = jnp.where(lane8[0:1] < 64, both[0:1], both[1:2])
         srhs[r - 1] = jnp.where(sub8 == 0, line, 0.0)
-    add_thin(thin_solve(), adj)
+    thin_a = thin_solve(False)
+    add_thin(thin_a, adj)
 
     def grad_row(r, carry):
         q = r - HALO
@@ -488,6 +533,8 @@
             settle(sent, warm_s.at[which, slot])
     settle(sent, cond_s)
     settle(gath.at[0 : 16 * (NSRCG - 1), :], src_s)
+    settle(thin_main.at[0 : 5 * XR], main_s)
+    settle(thin_edge, edge_s)
     settle(zbuf, z_s)
     settle(gbuf, g_s)
     settle(gt.at[:, 0 : 8 * (2 * NSRCG - 1), :], rs_s)
@@ -520,7 +567,11 @@
             pltpu.VMEM((128, 128), F32),
             pltpu.VMEM((XR, YR, 128), F32),
             pltpu.VMEM((128, EX * 128), BF16),
-            pltpu.VMEM((128, CX * YR), BF16),
+            pltpu.VMEM((4, XR, YR, 128), F32),
+            pltpu.VMEM((XR, 8, 128), F32),
+            pltpu.VMEM((2, 8, 128), F32),
+            thin,
+            pltpu.VMEM((2, 6, 8, 128), F32),
             thin,
             pltpu.VMEM((6, EX - 2, 8, 128), F32),
             inner, inner, thin, thin,
@@ -529,7 +580,8 @@
             pltpu.VMEM((NGY - 1, 8, 128), F32),
             pltpu.VMEM((2, 128, 128), F32),
             pltpu.VMEM((2, NSRCG, 16, 128), F32),
-            dma((5,)),
+            dma, dma, dma, dma,
+            dma((6,)),
             dma((2, 2)), dma((2, 2)),
             *([dma] * 10),
         ],

time: 58.5 us -> 57 us (0.974)
  Pallas kernels: 56.9 us -> 55.4 us
    pallas_call x1, Pallas kernels: 56.9 us -> 55.4 us  [body(): pl.pallas_call(kernel, out_shape=jax.ShapeDtypeStruct((xr, depth, yr), F3...]
where the time goes in v4:
time: 57 us; the launch traced here: 56.8 us
  Pallas kernels  55.4 us (97%)
  local copies, waits for them, and re-layouts  1.38 us (2%)
    pallas_call x1, Pallas kernels, body(): pl.pallas_call(kernel, out_shape=jax.ShapeDtypeStruct((xr, depth, yr), F3...  55.4 us
    unnamed x1, local copies, waits for them, and re-layouts  1.38 us

profile of v4, /device:TPU:1, one launch (start us, length us, event | category | flops | bytes accessed | tf_op | source)
XLA Modules:
  0.0 56.8 jit_solution(8802568455952342932)
XLA Ops:
  0.0 55.4 %shard_map.73 = f32[4,16,32]{2,1,0:T(8,128)} custom-call(f32[4,4,32,128]{3,2,1,0:T(8,128)} %wp_ref.1, f32[4,4,32,128]{3,2,1,0:T(8,128)} %wa_ref.1, f32[4,16,32]{2,1,0:T(8,128)} %bitcast.5, s32[2,32]{1,0:T(2,128)} %bitcast.6, s32[2,128]{1,0:T(2,128)} %bitcast.7, f32[32,128]{1,0:T(8,128)} %obs_hbm.1, s32[32]{0:T(128)} %order_hbm.1), custom_call_target="tpu_custom_call" | custom-call | tf_op jit(solution)/shard_map/pallas_call | solution.py:551
  55.4 1.4 %copy.9 = f32[4,32,16]{1,2,0:T(8,128)} copy(f32[4,32,16]{1,2,0:T(8,128)} %bitcast.4) | data formatting | bytes 16384

commit v5 on v4

--- a/solution.py
+++ b/solution.py
@@ -501,23 +501,21 @@
 
     pan8 = slope.at[0, :, 0:YR, :]
 
-    lax.fori_loop(HALO, HALO + CX, grad_row, 0, unroll=2)
     for c in range(2):
+        lax.fori_loop(HALO + XR * c, HALO + XR * c + XR, grad_row, 0, unroll=2)
         gt[c] = jnp.transpose(slope[0, XR * c : XR * c + XR, 0:YR, :].reshape(128, 128))
-
-    def rs_copy(ds, t):
-        c2 = core if t == 0 else 1 - core
-        s2 = lax.rem(src + ds, NSRCG)
-        return pltpu.make_async_remote_copy(
-            gt.at[c2, pl.ds(pl.multiple_of(16 * s2, 16), 16), :],
-            rbuf.at[t, ds],
-            rs_s, rs_r,
-            device_id=place(ds=ds, t=t), device_id_type=MESH,
-        )
-
-    copies_rs = [rs_copy(ds, t) for ds in range(NSRCG) for t in (0, 1) if ds or t]
-    for copy in copies_rs:
-        copy.start()
+        for ds in range(1, NSRCG):
+            s2 = lax.rem(src + ds, NSRCG)
+            pltpu.make_async_remote_copy(
+                gt.at[c, pl.ds(pl.multiple_of(16 * s2, 16), 16), :],
+                rbuf.at[lax.rem(core + c, 2), ds],
+                rs_s, rs_r,
+                device_id={"src": s2, "gx": 2 * zc + c, "gy": gy}, device_id_type=MESH,
+            ).start()
+    pltpu.make_async_remote_copy(
+        gt.at[1 - core, own_rows, :], rbuf.at[1, 0], rs_s, rs_r,
+        device_id=place(t=1), device_id_type=MESH,
+    ).start()
     pltpu.make_async_copy(gt.at[core, own_rows, :], rbuf.at[0, 0], rs_r).start()
     settle(rbuf, rs_r)
     total = rbuf[0, 0] + rbuf[1, 0]

time: 57 us -> 56.7 us (level)
  no operation moved by 1% of the time
where the time goes in v5:
time: 56.7 us; the launch traced here: 56.5 us
  Pallas kernels  55.1 us (97%)
  local copies, waits for them, and re-layouts  1.38 us (2%)
    pallas_call x1, Pallas kernels, body(): pl.pallas_call(kernel, out_shape=jax.ShapeDtypeStruct((xr, depth, yr), F3...  55.1 us
    unnamed x1, local copies, waits for them, and re-layouts  1.38 us

profile of v5, /device:TPU:1, one launch (start us, length us, event | category | flops | bytes accessed | tf_op | source)
XLA Modules:
  0.0 56.5 jit_solution(4120469306785577437)
XLA Ops:
  0.0 55.1 %shard_map.73 = f32[4,16,32]{2,1,0:T(8,128)} custom-call(f32[4,4,32,128]{3,2,1,0:T(8,128)} %wp_ref.1, f32[4,4,32,128]{3,2,1,0:T(8,128)} %wa_ref.1, f32[4,16,32]{2,1,0:T(8,128)} %bitcast.5, s32[2,32]{1,0:T(2,128)} %bitcast.6, s32[2,128]{1,0:T(2,128)} %bitcast.7, f32[32,128]{1,0:T(8,128)} %obs_hbm.1, s32[32]{0:T(128)} %order_hbm.1), custom_call_target="tpu_custom_call" | custom-call | tf_op jit(solution)/shard_map/pallas_call | solution.py:549
  55.1 1.4 %copy.9 = f32[4,32,16]{1,2,0:T(8,128)} copy(f32[4,32,16]{1,2,0:T(8,128)} %bitcast.4) | data formatting | bytes 16384
